TPU v7x, 32 devices: a whole 2x2x4 slice. The times are simulated.
32 devices in a mesh: slab: 16 (over z, y, core), sub: 2 (over x).
Axes of the slice: x: 2, y: 2, z: 4, core: 2. Of those that a mesh axis runs over, the one named last changes fastest.
Arguments:
- rhs_interior: float32 [16, 8, 2, 256, 128], P('slab', 'sub'), may hold values from -6 to 6
- rhs_separator: float32 [16, 2, 512, 128], P('slab'), may hold values from -6 to 6
- inverse_blocks: float32 [16, 8, 2, 256, 256], P('slab', 'sub'), may hold values from -0.375 to 0.375
- coupling: float32 [16, 8, 2, 512, 256], P('slab', 'sub'), may hold values from -0.0625 to 0.0625
- separator_rows: int32 [16, 8, 512], P('slab', 'sub'), may hold values from 0 to 511, each once within a row
- separator_inverse: float32 [16, 2, 512, 512], P('slab'), may hold values from -1.1 to 1.1
- transfer: float32 [16, 2, 512, 512], P('slab'), may hold values from -1.1 to 1.1
Outputs:
- interior_solution: float32 [16, 8, 2, 256, 128], P('slab', 'sub')
- separator_solution: float32 [16, 2, 512, 128], P('slab')
Inputs may be any that keep to these rules, and one draw needn't show every extreme that they name: Each block's separator_rows lists every separator row 0 to 511 exactly once.
All inputs are finite; a program needn't handle non-finite values.
Results may differ from a plain program's by a relative error of at most 0.0003.
Values sent between devices are 32-bit elements; how exact they have to be, the bound alone decides.
No kernel may reach another device: no remote copies, remote signals or barrier semaphores. Data moves between devices by JAX's collectives and lax.ppermute only.
A program may use at most 128 MiB of HBM per device.

v0:
```python
import jax
import jax.numpy as jnp
from jax import lax
from jax.experimental import pallas as pl
from jax.experimental.pallas import tpu as pltpu
from jax.sharding import PartitionSpec as P

GROUP = 4
RELAYED = 1
DIRECT = 1
AHEAD = 2
MIB = 1 << 20
LIGHT = pl.CostEstimate(flops=1, bytes_accessed=1, transcendentals=0)


def move(value, target):
    slabs, subs = lax.axis_size("slab"), lax.axis_size("sub")
    pairs = []
    for slab in range(slabs):
        for sub in range(subs):
            goal = target(slab, sub)
            if goal is not None:
                pairs.append((slab * subs + sub, goal[0] * subs + goal[1]))
    return lax.ppermute(value, ("slab", "sub"), pairs)


def swap(value, mask):
    return move(value, lambda slab, sub: (slab ^ mask, sub))


def shift_sub(value, steps):
    subs = lax.axis_size("sub")
    return move(value, lambda slab, sub: (slab, (sub + steps) % subs))


def pick(array, index):
    return lax.dynamic_index_in_dim(array, index, 0, keepdims=False)


def split(value):
    high = value.astype(jnp.bfloat16)
    return high, (value - high.astype(jnp.float32)).astype(jnp.bfloat16)


def dot(left, right):
    return jnp.dot(left, right, preferred_element_type=jnp.float32)


def dot_flipped(left, right):
    return lax.dot_general(left, right, (((1,), (1,)), ((), ())), preferred_element_type=jnp.float32)


def row_product(rows, matrix, slot, product):
    half = rows.shape[0] // 2
    size = rows.shape[1]
    high, low = split(rows)
    both = jnp.concatenate([high, low], axis=0)

    def against(start):
        wide = product(both, matrix[slot, 0, start : start + size])
        return wide[: 2 * half] + wide[2 * half :] + product(high, matrix[slot, 1, start : start + size])

    real, imag = against(0), against(size)
    return real + jnp.concatenate([-imag[half:], imag[:half]], axis=0)


def whole():
    return pl.BlockSpec(memory_space=pltpu.VMEM)


def plan(size, subs):
    step = 5 * size // 4 // RELAYED // subs
    direct = (2 * size - RELAYED * step * subs) // DIRECT
    return step, direct


def crossed_blocks(own, near):
    subs = lax.axis_size("sub")
    part = lax.axis_index("sub")
    step, direct = plan(own.shape[1], subs)
    shares = [
        lax.dynamic_slice_in_dim(own, (c * subs + part) * step, step, 0) for c in range(RELAYED)
    ]
    crossed = [swap(share, 2) for share in shares]
    start = RELAYED * subs * step
    for c in range(DIRECT):
        share, near = lax.optimization_barrier((own[start + c * direct : start + (c + 1) * direct], near))
        crossed.append(swap(share, 2))
    return crossed, near


def relayed_pieces(c, chunk):
    subs = lax.axis_size("sub")
    now = [chunk] + [shift_sub(chunk, k) for k in range(1, subs)]
    return [(c, k, piece) for k, piece in enumerate(now)]


def in_hbm(value):
    return pltpu.with_memory_space_constraint(value, pltpu.HBM)


def split_blocks(own, near, pieces, far, terms):
    subs = lax.axis_size("sub")
    size = own.shape[1]
    step, direct = plan(size, subs)
    values = [own, near] + [piece for _, _, piece in pieces] + list(far)
    count = len(pieces)

    def kernel(*refs):
        sources, (terms_ref, out, state) = refs[: len(values)], refs[len(values) : len(values) + 3]
        here = lax.axis_index("sub")
        member = lax.rem(lax.axis_index("slab"), GROUP)
        for slot in range(GROUP):
            value = terms_ref[(member ^ slot) * subs]
            for sub in range(1, subs):
                value = value + terms_ref[(member ^ slot) * subs + sub]
            state[slot] = value
        for i, source in enumerate(sources):
            if i < 2:
                out[i, 0], out[i, 1] = split(source[...])
                continue
            slot, (c, k, _) = 2 + (i - 2) // count, pieces[(i - 2) % count]
            if c < RELAYED:
                start = pl.multiple_of((c * subs + lax.rem(here - k + subs, subs)) * step, step)
                rows = pl.ds(start, step)
            else:
                start = RELAYED * subs * step + (c - RELAYED) * direct
                rows = pl.ds(start, direct)
            out[slot, 0, rows], out[slot, 1, rows] = split(source[...])

    return pl.pallas_call(
        kernel,
        out_shape=(
            pltpu.VMEM((GROUP, 2, 2 * size, size), jnp.bfloat16),
            jax.ShapeDtypeStruct((GROUP,) + terms.shape[1:], jnp.float32),
        ),
        in_specs=[whole()] * (len(values) + 1),
        out_specs=(whole(), whole()),
        compiler_params=pltpu.CompilerParams(vmem_limit_bytes=16 * MIB),
        name="split_blocks",
    )(*values, terms)


def near_dot(left, right):
    return dot(left[0], right[0]) + (dot(left[0], right[1]) + dot(left[1], right[0]))


def column_product(matrix, columns):
    half = columns.shape[1] // 2
    columns = split(columns)
    real = near_dot(split(matrix[0]), columns)
    imag = near_dot(split(matrix[1]), columns)
    return jnp.concatenate(
        [real[:, :half] - imag[:, half:], real[:, half:] + imag[:, :half]], axis=1
    )


def side_by_side(pair):
    return jnp.concatenate([pair[0], pair[1]], axis=1)


def spread_of(rows):
    count = rows.shape[1]
    place = lax.broadcasted_iota(jnp.int32, (count, count), 0)
    return jnp.where(rows == place, 1.0, 0.0).astype(jnp.bfloat16)


def spread_product(spread, columns):
    high, low = split(columns)
    return dot(spread, high) + dot(spread, low)


def separator_part(loads, lower, weights, rows, right, inverse):
    count, _, inner, shots = loads.shape
    size = right.shape[1]
    subs = lax.axis_size("sub")
    width = shots // (subs * GROUP)

    def kernel(load_hbm, lower_hbm, weight_hbm, rows_hbm, right_hbm, inverse_hbm, out, eliminated_hbm, *scratch):
        load_ref, lower_ref, weight_ref, right_ref, inverse_ref = scratch[:5]
        eliminated_ref, total, spread, rows_ref, arrived, right_arrived, inverse_arrived, rows_arrived, left = scratch[5:]

        def copies(b):
            sources = (load_hbm, lower_hbm, weight_hbm)
            rooms = (load_ref, lower_ref, weight_ref)
            return [
                pltpu.make_async_copy(source.at[b], room.at[b], arrived.at[i, b])
                for i, (source, room) in enumerate(zip(sources, rooms))
            ]

        def leaving(b):
            return pltpu.make_async_copy(eliminated_ref.at[b], eliminated_hbm.at[b], left.at[b])

        right_copy = pltpu.make_async_copy(right_hbm, right_ref, right_arrived)
        inverse_copy = pltpu.make_async_copy(inverse_hbm, inverse_ref, inverse_arrived)
        rows_copy = pltpu.make_async_copy(rows_hbm, rows_ref, rows_arrived)
        rows_copy.start()
        for b in range(min(AHEAD, count)):
            for copy in copies(b):
                copy.start()
        rows_copy.wait()
        for b in range(count):
            spread[b] = spread_of(rows_ref[b : b + 1])
        for b in range(count):
            for copy in copies(b):
                copy.wait()
            if b + AHEAD < count:
                for copy in copies(b + AHEAD):
                    copy.start()
            elif b + AHEAD == count:
                right_copy.start()
                inverse_copy.start()
            eliminated = column_product(lower_ref.at[b], side_by_side(load_ref.at[b]))
            eliminated_ref[b] = eliminated.T
            leaving(b).start()
            coupled = column_product(weight_ref.at[b], eliminated)
            load = spread_product(spread[b], coupled)
            total[...] = total[...] + load if b else load

        right_copy.wait()
        inverse_copy.wait()
        kept = jnp.where(lax.axis_index("sub") == 0, side_by_side(right_ref), 0.0)
        local = column_product(inverse_ref, kept - total[...])
        for half in range(2):
            shot_rows = local[:, half * shots : (half + 1) * shots].T
            for sub in range(subs):
                for member in range(GROUP):
                    start = (sub * GROUP + member) * width
                    out[member * subs + sub, half * width : (half + 1) * width] = shot_rows[
                        start : start + width
                    ]
        for b in range(count):
            leaving(b).wait()

    hbm = pl.BlockSpec(memory_space=pltpu.HBM)
    return pl.pallas_call(
        kernel,
        out_shape=(
            jax.ShapeDtypeStruct((GROUP * subs, 2 * width, size), jnp.float32),
            pltpu.HBM((count, 2 * shots, inner), jnp.float32),
        ),
        in_specs=[hbm] * 6,
        out_specs=(whole(), hbm),
        scratch_shapes=[pltpu.VMEM(value.shape, jnp.float32) for value in (loads, lower, weights, right, inverse)]
        + [
            pltpu.VMEM((count, 2 * shots, inner), jnp.float32),
            pltpu.VMEM((size, 2 * shots), jnp.float32),
            pltpu.VMEM((count, size, size), jnp.bfloat16),
            pltpu.VMEM(rows.shape, rows.dtype),
            pltpu.SemaphoreType.DMA((3, count)),
            pltpu.SemaphoreType.DMA,
            pltpu.SemaphoreType.DMA,
            pltpu.SemaphoreType.DMA,
            pltpu.SemaphoreType.DMA((count,)),
        ],
        compiler_params=pltpu.CompilerParams(vmem_limit_bytes=24 * MIB),
        cost_estimate=pl.CostEstimate(flops=40000000000, bytes_accessed=1 << 20, transcendentals=0),
        name="separator_part",
    )(*[in_hbm(value) for value in (loads, lower, weights, rows, right, inverse)])


def joined_blocks(before, lower, weights, rows, eliminated, chosen):
    count, _, size, inner = weights.shape
    shots = eliminated.shape[1] // 2

    def kernel(lower_hbm, weight_hbm, rows_ref, eliminated_hbm, *refs):
        joined_hbm, plain_hbm, lower_ref, weight_ref, eliminated_ref, joined_ref, plain_ref, arrived, left = refs[-9:]
        group = lax.div(lax.axis_index("slab"), GROUP)
        here = group == chosen[0]
        for other in chosen[1:]:
            here = jnp.logical_or(here, group == other)

        def copies(b):
            sources = (lower_hbm, weight_hbm, eliminated_hbm)
            rooms = (lower_ref, weight_ref, eliminated_ref)
            slot = lax.rem(b, 2)
            return [
                pltpu.make_async_copy(source.at[b], room.at[slot], arrived.at[i, slot])
                for i, (source, room) in enumerate(zip(sources, rooms))
            ]

        def leaving(b):
            slot = lax.rem(b, 2)
            return [
                pltpu.make_async_copy(joined_ref.at[slot], joined_hbm.at[b], left.at[0, slot]),
                pltpu.make_async_copy(plain_ref.at[slot], plain_hbm.at[b], left.at[1, slot]),
            ]

        @pl.when(here)
        def _():
            for copy in copies(0):
                copy.start()

            @pl.loop(0, count)
            def _(b):
                slot = lax.rem(b, 2)

                @pl.when(b + 1 < count)
                def _():
                    for copy in copies(b + 1):
                        copy.start()

                @pl.when(b >= 2)
                def _():
                    for copy in leaving(b - 2):
                        copy.wait()

                for copy in copies(b):
                    copy.wait()
                joined = column_product(weight_ref.at[slot], side_by_side(lower_ref.at[slot]))
                joined = spread_product(spread_of(rows_ref[pl.ds(b, 1)]), joined)
                for half in range(2):
                    high, low = split(joined[:, half * inner : (half + 1) * inner])
                    joined_ref[slot, half, 0] = high
                    joined_ref[slot, half, 1] = low
                rows_now = split(eliminated_ref[slot])
                real = near_dot(rows_now, split(lower_ref[slot, 0]))
                imag = near_dot(rows_now, split(lower_ref[slot, 1]))
                plain_ref[slot, :shots] = real[:shots] - imag[shots:]
                plain_ref[slot, shots:] = real[shots:] + imag[:shots]
                for copy in leaving(b):
                    copy.start()

            for b in range(max(0, count - 2), count):
                for copy in leaving(b):
                    copy.wait()

    hbm = pl.BlockSpec(memory_space=pltpu.HBM)
    operands = [in_hbm(lower), in_hbm(weights), rows, in_hbm(eliminated)]
    specs = [hbm, hbm, whole(), hbm]
    aliases = {}
    if before is not None:
        aliases = {4: 0, 5: 1}
        operands += [in_hbm(value) for value in before]
        specs += [hbm] * 2
    return pl.pallas_call(
        kernel,
        out_shape=(
            pltpu.HBM((count, 2, 2, size, inner), jnp.bfloat16),
            pltpu.HBM((count, 2 * shots, inner), jnp.float32),
        ),
        in_specs=specs,
        out_specs=(hbm, hbm),
        scratch_shapes=[
            pltpu.VMEM((2,) + lower.shape[1:], jnp.float32),
            pltpu.VMEM((2,) + weights.shape[1:], jnp.float32),
            pltpu.VMEM((2,) + eliminated.shape[1:], jnp.float32),
            pltpu.VMEM((2, 2, 2, size, inner), jnp.bfloat16),
            pltpu.VMEM((2, 2 * shots, inner), jnp.float32),
            pltpu.SemaphoreType.DMA((3, 2)),
            pltpu.SemaphoreType.DMA((2, 2)),
        ],
        input_output_aliases=aliases,
        compiler_params=pltpu.CompilerParams(vmem_limit_bytes=12 * MIB),
        cost_estimate=LIGHT,
        name="joined_blocks",
    )(*operands)


def finish(arrived, joined, plain):
    count, _, _, size, inner = joined.shape
    pieces, height, _ = arrived.shape
    subs = pieces // GROUP
    width = height // 2
    shots = pieces * width

    def kernel(arrived_ref, joined_hbm, plain_hbm, interior_out, solution_out, joined_ref, plain_ref, solved, landed):
        block = pl.program_id(0)

        def copies(b):
            return [
                pltpu.make_async_copy(joined_hbm.at[b], joined_ref.at[b], landed.at[0, b]),
                pltpu.make_async_copy(plain_hbm.at[b], plain_ref.at[b], landed.at[1, b]),
            ]

        @pl.when(block == 0)
        def _():
            for b in range(count):
                for copy in copies(b):
                    copy.start()
            for half in range(2):
                for sub in range(subs):
                    for member in range(GROUP):
                        start = half * shots + (sub * GROUP + member) * width
                        solved[start : start + width] = arrived_ref[
                            member * subs + sub, half * width : (half + 1) * width
                        ]
                solution_out[half] = solved[half * shots : (half + 1) * shots].T

        for copy in copies(block):
            copy.wait()
        rows_now = split(solved[...])
        real = near_dot(rows_now, (joined_ref[block, 0, 0], joined_ref[block, 0, 1]))
        imag = near_dot(rows_now, (joined_ref[block, 1, 0], joined_ref[block, 1, 1]))
        interior_out[0, 0] = (plain_ref[block, :shots] - (real[:shots] - imag[shots:])).T
        interior_out[0, 1] = (plain_ref[block, shots:] - (real[shots:] + imag[:shots])).T

    hbm = pl.BlockSpec(memory_space=pltpu.HBM)
    return pl.pallas_call(
        kernel,
        grid=(count,),
        out_shape=(
            jax.ShapeDtypeStruct((count, 2, inner, shots), jnp.float32),
            jax.ShapeDtypeStruct((2, size, shots), jnp.float32),
        ),
        in_specs=[whole(), hbm, hbm],
        out_specs=(
            pl.BlockSpec((1, 2, inner, shots), lambda b: (b, 0, 0, 0)),
            pl.BlockSpec((2, size, shots), lambda b: (0, 0, 0)),
        ),
        scratch_shapes=[
            pltpu.VMEM(joined.shape, joined.dtype),
            pltpu.VMEM(plain.shape, plain.dtype),
            pltpu.VMEM((2 * shots, size), jnp.float32),
            pltpu.SemaphoreType.DMA((2, count)),
        ],
        compiler_params=pltpu.CompilerParams(vmem_limit_bytes=16 * MIB),
        name="finish",
    )(arrived, in_hbm(joined), in_hbm(plain))


def turn(state, answer, incoming, blocks, group, forward, backward):
    shape = state.shape[1:]
    subs = answer.shape[1]

    def kernel(*refs):
        state_in, _, block_ref = refs[:3]
        incoming_ref = None if incoming is None else refs[3]
        state_out, answer_out, _, carry = refs[-4:]
        position = lax.axis_index("slab")
        member = lax.rem(position, GROUP)

        @pl.when(lax.div(position, GROUP) == group)
        def _():
            value = None if incoming is None else incoming_ref[...]
            if forward:
                for i in range(GROUP):
                    slot = member ^ i
                    local = state_in[slot]
                    if value is None:
                        value = local
                    else:
                        value = local - row_product(value, block_ref, slot, dot_flipped)
                    state_out[slot] = value
                carry[...] = value
            if backward:
                value = None if forward else value
                for i in reversed(range(GROUP)):
                    slot = member ^ i
                    trace = state_out[slot] if forward else state_in[slot]
                    value = trace if value is None else trace - value
                    for sub in range(subs):
                        answer_out[i, sub] = value
                    if i or group:
                        value = row_product(value, block_ref, slot, dot)
                carry[...] = value

    operands = (state, answer, blocks) + (() if incoming is None else (incoming,))
    return pl.pallas_call(
        kernel,
        out_shape=(
            jax.ShapeDtypeStruct(state.shape, jnp.float32),
            jax.ShapeDtypeStruct(answer.shape, jnp.float32),
            pltpu.VMEM(blocks.shape, blocks.dtype),
            jax.ShapeDtypeStruct(shape, jnp.float32),
        ),
        in_specs=[whole()] * len(operands),
        out_specs=(whole(),) * 4,
        input_output_aliases={0: 0, 1: 1, 2: 2},
        compiler_params=pltpu.CompilerParams(vmem_limit_bytes=16 * MIB),
        name="sweep_turn",
    )(*operands)


def body(
    rhs_interior,
    rhs_separator,
    inverse_blocks,
    coupling,
    separator_rows,
    separator_inverse,
    transfer,
):
    slabs, subs = lax.axis_size("slab"), lax.axis_size("sub")
    member = lax.rem(lax.axis_index("slab"), GROUP)
    turns = slabs // GROUP
    loads, lower, weights, rows = rhs_interior[0], inverse_blocks[0], coupling[0], separator_rows[0]
    groups = [
        [(g * GROUP + m) * subs + u for m in range(GROUP) for u in range(subs)] for g in range(turns)
    ]

    def exchange(value):
        return lax.all_to_all(value, ("slab", "sub"), 0, 0, axis_index_groups=groups, tiled=True)

    own = transfer[0].reshape(-1, transfer.shape[-1])
    crossed, near = crossed_blocks(own, swap(own, 1))
    near, rows = lax.optimization_barrier((near, rows))
    terms, eliminated = separator_part(
        loads, lower, weights, rows, rhs_separator[0], separator_inverse[0]
    )
    crossed[:RELAYED], terms = lax.optimization_barrier((crossed[:RELAYED], terms))
    pieces = [piece for c in range(RELAYED) for piece in relayed_pieces(c, crossed[c])]
    pieces += [(c, 0, crossed[c]) for c in range(RELAYED, RELAYED + DIRECT)]
    terms = exchange(terms)
    early = [swap(piece, 1) if k == 0 and c < RELAYED else None for c, k, piece in pieces]
    settled, terms = lax.optimization_barrier(([piece for _, _, piece in pieces], terms))
    pieces = [(c, k, piece) for (c, k, _), piece in zip(pieces, settled)]
    far = [swap(piece, 1) if sent is None else sent for piece, sent in zip(settled, early)]
    blocks, state = split_blocks(own, near, pieces, far, terms)

    def hop(value, source, steps):
        return move(
            value,
            lambda slab, sub: (slab + GROUP * steps, sub) if slab // GROUP == source else None,
        )

    incoming = joined = None
    answer = jnp.zeros((GROUP, subs) + state.shape[1:], jnp.float32)
    for group in range(turns):
        last = group == turns - 1
        state, answer, blocks, carry = turn(state, answer, incoming, blocks, group, True, last)
        if not last:
            incoming = hop(carry, group, 1)
    for group in reversed(range(turns - 1)):
        incoming = hop(carry, group + 1, -1)
        if group >= turns - 3:
            carry, eliminated = lax.optimization_barrier((carry, eliminated))
            late = group == turns - 3
            chosen = [turns - 2] if late else [g for g in range(turns) if g != turns - 2]
            joined = joined_blocks(joined, lower, weights, rows, eliminated, chosen)
            state, joined = lax.optimization_barrier((state, joined))
        state, answer, blocks, carry = turn(state, answer, incoming, blocks, group, False, True)

    arrived = exchange(answer.reshape((GROUP * subs,) + answer.shape[2:]))
    interior, solved = finish(arrived, *joined)
    return (interior[None], solved[None])


def solution(mesh):
    in_specs = (
        P("slab", "sub", None, None, None),
        P("slab", None, None, None),
        P("slab", "sub", None, None, None),
        P("slab", "sub", None, None, None),
        P("slab", "sub", None),
        P("slab", None, None, None),
        P("slab", None, None, None),
    )
    out_specs = (P("slab", "sub", None, None, None), P("slab", None, None, None))
    return jax.shard_map(body, mesh=mesh, in_specs=in_specs, out_specs=out_specs, check_vma=False)
```

profile of v0, /device:TPU:0, one launch (start us, length us, event | category | flops | bytes accessed | tf_op | source)
XLA Modules:
  0.0 111.2 jit_solution(1647335248891040598)
XLA Ops:
  1.1 1.1 %constant_dynamic-slice_fusion = f32[320,512]{1,0:T(8,128)S(1)} fusion(f32[1024,512]{1,0:T(8,128)} %bitcast.12, s32[]{:T(128)S(6)} %select_n.3), kind=kLoop, calls=%fused_computation | loop fusion | bytes 1310724 | tf_op jit(solution)/shard_map/dynamic_slice | solution.py:82
  2.3 2.6 %collective-permute-start.1 = (f32[320,512]{1,0:T(8,128)S(1)}, f32[320,512]{1,0:T(8,128)S(1)}, u32[]{:S(2)}, u32[]{:S(2)}) collective-permute-start(f32[320,512]{1,0:T(8,128)S(1)} %constant_dynamic-slice_fusion), channel_id=1, source_target_pairs={{0,4},{1,5},{2,6},{3,7},{4,0},{5,1},{6,2},{7,3},{8,12},{9,13},{10,... | collective-permute-start | bytes 1966088 | tf_op jit(solution)/shard_map/ppermute | solution.py:24
  4.9 1.2 %slice.4 = f32[384,512]{1,0:T(8,128)S(1)} slice(f32[1024,512]{1,0:T(8,128)} %bitcast.13), slice={[640:1024], [0:512]} | slice | bytes 1572864 | tf_op jit(solution)/shard_map/slice | solution.py:87
  6.1 1.9 %collective-permute-start.3 = (f32[384,512]{1,0:T(8,128)S(1)}, f32[384,512]{1,0:T(8,128)S(1)}, u32[]{:S(2)}, u32[]{:S(2)}) collective-permute-start(f32[384,512]{1,0:T(8,128)S(1)} %slice.4), channel_id=1, source_target_pairs={{0,4},{1,5},{2,6},{3,7},{4,0},{5,1},{6,2},{7,3},{8,12},{9,13},{10,... | collective-permute-start | bytes 2359304 | tf_op jit(solution)/shard_map/ppermute | solution.py:24
  8.0 10.9 %separator_part.1 = (f32[8,32,512]{2,1,0:T(8,128)S(1)}, f32[4,256,256]{2,1,0:T(8,128)}) custom-call(f32[4,2,256,128]{3,2,1,0:T(8,128)} %bitcast.25, f32[4,2,256,256]{3,2,1,0:T(8,128)} %bitcast.21, f32[4,2,512,256]{3,2,1,0:T(8,128)} %bitcast.18, s32[4,512]{1,0:T(4,128)} %bitcast.15, f32[2,512,128]{2,1,0:T(8,128)} %bitcast.27, f32[2,512,512]{2,1,0:T(8,128)} %bitcast.24), custom_call_target="tpu_custom_call" | custom-call | flops 40000000000 | bytes 1048576 | tf_op jit(solution)/shard_map/separator_part/pallas_call | solution.py:236
  18.9 1.6 %collective-permute-done.1.refs_2_ = f32[320,512]{1,0:T(8,128)S(1)} collective-permute-done((f32[320,512]{1,0:T(8,128)S(1)}, f32[320,512]{1,0:T(8,128)S(1)}, u32[]{:S(2)}, u32[]{:S(2)}) %collective-permute-start.1) | collective-permute-done | bytes 655392 | tf_op jit(solution)/shard_map/ppermute | solution.py:24
  20.5 1.9 %collective-permute-start.2 = (f32[320,512]{1,0:T(8,128)S(1)}, f32[320,512]{1,0:T(8,128)S(1)}, u32[]{:S(2)}, u32[]{:S(2)}) collective-permute-start(f32[320,512]{1,0:T(8,128)S(1)} %collective-permute-done.1.refs_2_), channel_id=1, source_target_pairs={{0,1},{1,0},{2,3},{3,2},{4,5},{5,4},{6,7},{7,6},{8,9},{9,8},{10,11... | collective-permute-start | bytes 1966088 | tf_op jit(solution)/shard_map/ppermute | solution.py:24
  22.4 20.3 %all_to_all.10.refs_8_ = f32[8,32,512]{2,1,0:T(8,128)S(1)} all-to-all(f32[8,32,512]{2,1,0:T(8,128)S(1)} %get-tuple-element.61), channel_id=1, replica_groups={{0,1,2,3,4,5,6,7},{8,9,10,11,12,13,14,15},{16,17,18,19,20,21,22,23},{24..., dimensions={0} | all-to-all | bytes 1048576 | tf_op jit(solution)/shard_map/all_to_all | solution.py:493
  43.4 2.5 %collective-permute-done.4.refs_5_ = f32[320,512]{1,0:T(8,128)S(1)} collective-permute-done((f32[320,512]{1,0:T(8,128)S(1)}, f32[320,512]{1,0:T(8,128)S(1)}, u32[]{:S(2)}, u32[]{:S(2)}) %collective-permute-start.4) | collective-permute-done | bytes 655392 | tf_op jit(solution)/shard_map/ppermute | solution.py:24
  45.9 0.9 collective-permute-done.5.refs_6_
  46.9 1.2 %split_blocks.1 = (bf16[4,2,1024,512]{3,2,1,0:T(8,128)(2,1)S(1)}, f32[4,32,512]{2,1,0:T(8,128)S(1)}) custom-call(f32[1024,512]{1,0:T(8,128)S(1)} %bitcast.14, f32[1024,512]{1,0:T(8,128)S(1)} %collective-permute-done.refs_1_, f32[320,512]{1,0:T(8,128)S(1)} %collective-permute-done.1.refs_2_, f32[320,512]{1,0:T(8,128)S(1)} %collective-permute-done.2.refs_3_, ...), custom_call_target="tpu_custom_call" | custom-call | tf_op jit(solution)/shard_map/split_blocks/pallas_call | solution.py:131
  48.1 2.1 %sweep_turn.7 = (f32[4,32,512]{2,1,0:T(8,128)S(1)}, f32[4,2,32,512]{3,2,1,0:T(8,128)S(1)}, bf16[4,2,1024,512]{3,2,1,0:T(8,128)(2,1)S(1)}, f32[32,512]{1,0:T(8,128)S(1)}) custom-call(f32[4,32,512]{2,1,0:T(8,128)S(1)} %get-tuple-element.66.refs_0_, ...), custom_call_target="tpu_custom_call", output_to_operand_aliasing={{0}: (0, {}), {1}: (1, {}), {2}: (2, {})} | custom-call | tf_op jit(solution)/shard_map/sweep_turn/pallas_call | solution.py:459
  50.2 1.4 %collective-permute-start.7 = (f32[32,512]{1,0:T(8,128)S(1)}, f32[32,512]{1,0:T(8,128)S(1)}, u32[]{:S(2)}, u32[]{:S(2)}) collective-permute-start(f32[32,512]{1,0:T(8,128)S(1)} %get-tuple-element.71), channel_id=1, source_target_pairs={{0,8},{1,9},{2,10},{3,11},{4,12},{5,13},{6,14},{7,15}} | collective-permute-start | bytes 196616 | tf_op jit(solution)/shard_map/ppermute | solution.py:24
  51.7 1.9 %collective-permute-done.7.refs_3_ = f32[32,512]{1,0:T(8,128)S(1)} collective-permute-done((f32[32,512]{1,0:T(8,128)S(1)}, f32[32,512]{1,0:T(8,128)S(1)}, u32[]{:S(2)}, u32[]{:S(2)}) %collective-permute-start.7) | collective-permute-done | bytes 65568 | tf_op jit(solution)/shard_map/ppermute | solution.py:24
  53.6 0.7 collective-permute-start.8
  54.3 0.7 collective-permute-start.9
  55.2 0.7 collective-permute-start.10
  55.8 10.0 %joined_blocks.2 = (bf16[4,2,2,512,256]{4,3,2,1,0:T(8,128)(2,1)}, f32[4,256,256]{2,1,0:T(8,128)}) custom-call(f32[4,2,256,256]{3,2,1,0:T(8,128)} %bitcast.22, f32[4,2,512,256]{3,2,1,0:T(8,128)} %bitcast.19, s32[4,512]{1,0:T(4,128)S(1)} %bitcast.16, f32[4,256,256]{2,1,0:T(8,128)} %get-tuple-element.91.eliminated_hbm), custom_call_target="tpu_custom_call" | custom-call | flops 1 | bytes 1 | tf_op jit(solution)/shard_map/joined_blocks/pallas_call | solution.py:336
  65.9 0.7 collective-permute-start.11
  66.7 1.3 %collective-permute-start.12 = (f32[32,512]{1,0:T(8,128)S(1)}, f32[32,512]{1,0:T(8,128)S(1)}, u32[]{:S(2)}, u32[]{:S(2)}) collective-permute-start(f32[32,512]{1,0:T(8,128)S(1)} %get-tuple-element.102), channel_id=1, source_target_pairs={{8,0},{9,1},{10,2},{11,3},{12,4},{13,5},{14,6},{15,7}} | collective-permute-start | bytes 196616 | tf_op jit(solution)/shard_map/ppermute | solution.py:24
  68.0 23.2 %collective-permute-done.12.refs_3_ = f32[32,512]{1,0:T(8,128)S(1)} collective-permute-done((f32[32,512]{1,0:T(8,128)S(1)}, f32[32,512]{1,0:T(8,128)S(1)}, u32[]{:S(2)}, u32[]{:S(2)}) %collective-permute-start.12) | collective-permute-done | bytes 65568 | tf_op jit(solution)/shard_map/ppermute | solution.py:24
  91.2 2.0 %sweep_turn.13 = (f32[4,32,512]{2,1,0:T(8,128)S(1)}, f32[4,2,32,512]{3,2,1,0:T(8,128)S(1)}, bf16[4,2,1024,512]{3,2,1,0:T(8,128)(2,1)S(1)}, f32[32,512]{1,0:T(8,128)}) custom-call(f32[4,32,512]{2,1,0:T(8,128)S(1)} %get-tuple-element.99.refs_0_, ...), custom_call_target="tpu_custom_call", output_to_operand_aliasing={{0}: (0, {}), {1}: (1, {}), {2}: (2, {})} | custom-call | tf_op jit(solution)/shard_map/sweep_turn/pallas_call | solution.py:459
  93.2 13.0 %all_to_all.11.arrived_ref = f32[8,32,512]{2,1,0:T(8,128)S(1)} all-to-all(f32[8,32,512]{2,1,0:T(8,128)S(1)} %bitcast.10), channel_id=1, replica_groups={{0,1,2,3,4,5,6,7},{8,9,10,11,12,13,14,15},{16,17,18,19,20,21,22,23},{24..., dimensions={0} | all-to-all | bytes 1048576 | tf_op jit(solution)/shard_map/all_to_all | solution.py:493
  106.2 4.8 %finish.1 = (f32[4,2,256,128]{3,2,1,0:T(8,128)}, f32[2,512,128]{2,1,0:T(8,128)}) custom-call(f32[8,32,512]{2,1,0:T(8,128)S(1)} %all_to_all.11.arrived_ref, bf16[4,2,2,512,256]{4,3,2,1,0:T(8,128)(2,1)} %get-tuple-element.104.joined_hbm, f32[4,256,256]{2,1,0:T(8,128)} %get-tuple-element.105.plain_hbm), custom_call_target="tpu_custom_call" | custom-call | tf_op jit(solution)/shard_map/finish/pallas_call | solution.py:399
  (23 shorter events, 1.7 us)
Async XLA Ops:
  0.6 5.4 %collective-permute-start = (f32[1024,512]{1,0:T(8,128)}, f32[1024,512]{1,0:T(8,128)S(1)}, u32[]{:S(2)}, u32[]{:S(2)}) collective-permute-start(f32[1024,512]{1,0:T(8,128)} %bitcast.11), channel_id=1, source_target_pairs={{0,2},{1,3},{2,0},{3,1},{4,6},{5,7},{6,4},{7,5},{8,10},{9,11},{10,... | collective-permute-start | bytes 6291464 | tf_op jit(solution)/shard_map/ppermute | solution.py:24
  2.3 18.2 %collective-permute-start.1 = (f32[320,512]{1,0:T(8,128)S(1)}, f32[320,512]{1,0:T(8,128)S(1)}, u32[]{:S(2)}, u32[]{:S(2)}) collective-permute-start(f32[320,512]{1,0:T(8,128)S(1)} %constant_dynamic-slice_fusion), channel_id=1, source_target_pairs={{0,4},{1,5},{2,6},{3,7},{4,0},{5,1},{6,2},{7,3},{8,12},{9,13},{10,... | collective-permute-start | bytes 1966088 | tf_op jit(solution)/shard_map/ppermute | solution.py:24
  6.1 36.6 %collective-permute-start.3 = (f32[384,512]{1,0:T(8,128)S(1)}, f32[384,512]{1,0:T(8,128)S(1)}, u32[]{:S(2)}, u32[]{:S(2)}) collective-permute-start(f32[384,512]{1,0:T(8,128)S(1)} %slice.4), channel_id=1, source_target_pairs={{0,4},{1,5},{2,6},{3,7},{4,0},{5,1},{6,2},{7,3},{8,12},{9,13},{10,... | collective-permute-start | bytes 2359304 | tf_op jit(solution)/shard_map/ppermute | solution.py:24
  8.0 38.8 %copy-start = (f32[1,2,512,512]{3,2,1,0:T(8,128)S(1)}, f32[1,2,512,512]{3,2,1,0:T(8,128)}, u32[]{:S(2)}) copy-start(f32[1,2,512,512]{3,2,1,0:T(8,128)} %param.13) | copy-start | bytes 6291460
  20.5 22.2 %collective-permute-start.2 = (f32[320,512]{1,0:T(8,128)S(1)}, f32[320,512]{1,0:T(8,128)S(1)}, u32[]{:S(2)}, u32[]{:S(2)}) collective-permute-start(f32[320,512]{1,0:T(8,128)S(1)} %collective-permute-done.1.refs_2_), channel_id=1, source_target_pairs={{0,1},{1,0},{2,3},{3,2},{4,5},{5,4},{6,7},{7,6},{8,9},{9,8},{10,11... | collective-permute-start | bytes 1966088 | tf_op jit(solution)/shard_map/ppermute | solution.py:24
  42.7 4.2 %collective-permute-start.6 = (f32[384,512]{1,0:T(8,128)S(1)}, f32[384,512]{1,0:T(8,128)S(1)}, u32[]{:S(2)}, u32[]{:S(2)}) collective-permute-start(f32[384,512]{1,0:T(8,128)S(1)} %collective-permute-done.3.refs_4_), channel_id=1, source_target_pairs={{0,2},{1,3},{2,0},{3,1},{4,6},{5,7},{6,4},{7,5},{8,10},{9,11},{10,... | collective-permute-start | bytes 2359304 | tf_op jit(solution)/shard_map/ppermute | solution.py:24
  42.9 3.1 %collective-permute-start.4 = (f32[320,512]{1,0:T(8,128)S(1)}, f32[320,512]{1,0:T(8,128)S(1)}, u32[]{:S(2)}, u32[]{:S(2)}) collective-permute-start(f32[320,512]{1,0:T(8,128)S(1)} %collective-permute-done.1.refs_2_), channel_id=1, source_target_pairs={{0,2},{1,3},{2,0},{3,1},{4,6},{5,7},{6,4},{7,5},{8,10},{9,11},{10,... | collective-permute-start | bytes 1966088 | tf_op jit(solution)/shard_map/ppermute | solution.py:24
  43.2 3.6 %collective-permute-start.5 = (f32[320,512]{1,0:T(8,128)S(1)}, f32[320,512]{1,0:T(8,128)S(1)}, u32[]{:S(2)}, u32[]{:S(2)}) collective-permute-start(f32[320,512]{1,0:T(8,128)S(1)} %collective-permute-done.2.refs_3_), channel_id=1, source_target_pairs={{0,2},{1,3},{2,0},{3,1},{4,6},{5,7},{6,4},{7,5},{8,10},{9,11},{10,... | collective-permute-start | bytes 1966088 | tf_op jit(solution)/shard_map/ppermute | solution.py:24
  50.2 3.3 %collective-permute-start.7 = (f32[32,512]{1,0:T(8,128)S(1)}, f32[32,512]{1,0:T(8,128)S(1)}, u32[]{:S(2)}, u32[]{:S(2)}) collective-permute-start(f32[32,512]{1,0:T(8,128)S(1)} %get-tuple-element.71), channel_id=1, source_target_pairs={{0,8},{1,9},{2,10},{3,11},{4,12},{5,13},{6,14},{7,15}} | collective-permute-start | bytes 196616 | tf_op jit(solution)/shard_map/ppermute | solution.py:24
  53.6 0.7 collective-permute-start.8
  54.2 1.6 %copy-start.1 = (s32[1,4,512]{2,1,0:T(4,128)S(1)}, s32[1,4,512]{2,1,0:T(4,128)}, u32[]{:S(2)}) copy-start(s32[1,4,512]{2,1,0:T(4,128)} %param.11) | copy-start | bytes 24580
  54.3 0.7 collective-permute-start.9
  55.2 10.7 %collective-permute-start.10 = (f32[32,512]{1,0:T(8,128)S(1)}, f32[32,512]{1,0:T(8,128)S(1)}, u32[]{:S(2)}, u32[]{:S(2)}) collective-permute-start(f32[32,512]{1,0:T(8,128)S(1)} %get-tuple-element.81), channel_id=1, source_target_pairs={{24,16},{25,17},{26,18},{27,19},{28,20},{29,21},{30,22},{31,23}} | collective-permute-start | bytes 196616 | tf_op jit(solution)/shard_map/ppermute | solution.py:24
  65.9 0.8 collective-permute-start.11
  66.7 24.5 %collective-permute-start.12 = (f32[32,512]{1,0:T(8,128)S(1)}, f32[32,512]{1,0:T(8,128)S(1)}, u32[]{:S(2)}, u32[]{:S(2)}) collective-permute-start(f32[32,512]{1,0:T(8,128)S(1)} %get-tuple-element.102), channel_id=1, source_target_pairs={{8,0},{9,1},{10,2},{11,3},{12,4},{13,5},{14,6},{15,7}} | collective-permute-start | bytes 196616 | tf_op jit(solution)/shard_map/ppermute | solution.py:24
where the time goes:
time: 112 us; the launch traced here: 111 us
  blocking collectives  33.3 us (30%)
  Pallas kernels  31.3 us (28%)
  waiting for transfers between devices  30.2 us (27%)
  starting transfers between devices  13 us (12%)
  local copies, waits for them, and re-layouts  2.37 us (2%)
    all_to_all x2, blocking collectives, exchange(): lax.all_to_all(value, ('slab', 'sub'), 0, 0, axis_index_groups=groups, ti...  33.3 us
    ppermute x13, waiting for transfers between devices, move(): return lax.ppermute(value, ('slab', 'sub'), pairs)  30.2 us
    ppermute x13, starting transfers between devices, move(): return lax.ppermute(value, ('slab', 'sub'), pairs)  13 us
    pallas_call x1, Pallas kernels, separator_part(): pl.pallas_call(kernel, out_shape=(jax.ShapeDtypeStruct((GROUP * subs, 2 *...  10.9 us
    pallas_call x2, Pallas kernels, joined_blocks(): pl.pallas_call(kernel, out_shape=(pltpu.HBM((count, 2, 2, size, inner), j...  10.1 us
    pallas_call x1, Pallas kernels, finish(): pl.pallas_call(kernel, grid=(count,), out_shape=(jax.ShapeDtypeStruct((co...  4.82 us
    pallas_call x7, Pallas kernels, turn(): pl.pallas_call(kernel, out_shape=(jax.ShapeDtypeStruct(state.shape, jnp.f...  4.34 us
  transfers between devices with their start and end apart: 13, of which 5 were waited for; matrix products, arithmetic and copies ran while one was open for 2% of the time, Pallas kernels for 19%

commit v1 on v0

--- a/solution.py
+++ b/solution.py
@@ -259,16 +259,15 @@
     )(*[in_hbm(value) for value in (loads, lower, weights, rows, right, inverse)])
 
 
-def joined_blocks(before, lower, weights, rows, eliminated, chosen):
+def joined_blocks(before, lower, weights, rows, eliminated, turns):
     count, _, size, inner = weights.shape
     shots = eliminated.shape[1] // 2
 
     def kernel(lower_hbm, weight_hbm, rows_ref, eliminated_hbm, *refs):
         joined_hbm, plain_hbm, lower_ref, weight_ref, eliminated_ref, joined_ref, plain_ref, arrived, left = refs[-9:]
-        group = lax.div(lax.axis_index("slab"), GROUP)
-        here = group == chosen[0]
-        for other in chosen[1:]:
-            here = jnp.logical_or(here, group == other)
+        halves = lax.div(lax.axis_index("slab"), GROUP) == turns - 2
+        first = 0 if before is None else count // 2
+        last = jnp.where(halves == (before is None), count // 2, count)
 
         def copies(b):
             sources = (lower_hbm, weight_hbm, eliminated_hbm)
@@ -286,21 +285,21 @@
                 pltpu.make_async_copy(plain_ref.at[slot], plain_hbm.at[b], left.at[1, slot]),
             ]
 
-        @pl.when(here)
+        @pl.when(last > first)
         def _():
-            for copy in copies(0):
+            for copy in copies(first):
                 copy.start()
 
-            @pl.loop(0, count)
+            @pl.loop(first, last)
             def _(b):
                 slot = lax.rem(b, 2)
 
-                @pl.when(b + 1 < count)
+                @pl.when(b + 1 < last)
                 def _():
                     for copy in copies(b + 1):
                         copy.start()
 
-                @pl.when(b >= 2)
+                @pl.when(b >= first + 2)
                 def _():
                     for copy in leaving(b - 2):
                         copy.wait()
@@ -321,7 +320,8 @@
                 for copy in leaving(b):
                     copy.start()
 
-            for b in range(max(0, count - 2), count):
+            @pl.loop(jnp.maximum(first, last - 2), last)
+            def _(b):
                 for copy in leaving(b):
                     copy.wait()
 
@@ -364,20 +364,11 @@
     width = height // 2
     shots = pieces * width
 
-    def kernel(arrived_ref, joined_hbm, plain_hbm, interior_out, solution_out, joined_ref, plain_ref, solved, landed):
+    def kernel(arrived_ref, joined_ref, plain_ref, interior_out, solution_out, solved):
         block = pl.program_id(0)
-
-        def copies(b):
-            return [
-                pltpu.make_async_copy(joined_hbm.at[b], joined_ref.at[b], landed.at[0, b]),
-                pltpu.make_async_copy(plain_hbm.at[b], plain_ref.at[b], landed.at[1, b]),
-            ]
 
         @pl.when(block == 0)
         def _():
-            for b in range(count):
-                for copy in copies(b):
-                    copy.start()
             for half in range(2):
                 for sub in range(subs):
                     for member in range(GROUP):
@@ -387,15 +378,12 @@
                         ]
                 solution_out[half] = solved[half * shots : (half + 1) * shots].T
 
-        for copy in copies(block):
-            copy.wait()
         rows_now = split(solved[...])
         real = near_dot(rows_now, (joined_ref[block, 0, 0], joined_ref[block, 0, 1]))
         imag = near_dot(rows_now, (joined_ref[block, 1, 0], joined_ref[block, 1, 1]))
         interior_out[0, 0] = (plain_ref[block, :shots] - (real[:shots] - imag[shots:])).T
         interior_out[0, 1] = (plain_ref[block, shots:] - (real[shots:] + imag[:shots])).T
 
-    hbm = pl.BlockSpec(memory_space=pltpu.HBM)
     return pl.pallas_call(
         kernel,
         grid=(count,),
@@ -403,29 +391,50 @@
             jax.ShapeDtypeStruct((count, 2, inner, shots), jnp.float32),
             jax.ShapeDtypeStruct((2, size, shots), jnp.float32),
         ),
-        in_specs=[whole(), hbm, hbm],
+        in_specs=[whole()] * 3,
         out_specs=(
             pl.BlockSpec((1, 2, inner, shots), lambda b: (b, 0, 0, 0)),
             pl.BlockSpec((2, size, shots), lambda b: (0, 0, 0)),
         ),
         scratch_shapes=[
-            pltpu.VMEM(joined.shape, joined.dtype),
-            pltpu.VMEM(plain.shape, plain.dtype),
             pltpu.VMEM((2 * shots, size), jnp.float32),
-            pltpu.SemaphoreType.DMA((2, count)),
         ],
         compiler_params=pltpu.CompilerParams(vmem_limit_bytes=16 * MIB),
         name="finish",
-    )(arrived, in_hbm(joined), in_hbm(plain))
-
-
-def turn(state, answer, incoming, blocks, group, forward, backward):
+    )(arrived, joined, plain)
+
+
+def flip_blocks(blocks):
+    size = blocks.shape[-1]
+
+    def kernel(blocks_ref, out):
+        @pl.when(lax.axis_index("slab") >= GROUP)
+        def _():
+            @pl.loop(0, 4 * GROUP)
+            def _(i):
+                slot, part, half = lax.div(i, 4), lax.rem(lax.div(i, 2), 2), lax.rem(i, 2)
+                rows = pl.ds(pl.multiple_of(half * size, size), size)
+                out[slot, part, rows] = blocks_ref[slot, part, rows].T
+
+    return pl.pallas_call(
+        kernel,
+        out_shape=pltpu.VMEM(blocks.shape, blocks.dtype),
+        in_specs=[whole()],
+        out_specs=whole(),
+        compiler_params=pltpu.CompilerParams(vmem_limit_bytes=12 * MIB),
+        cost_estimate=LIGHT,
+        name="flip_blocks",
+    )(blocks)
+
+
+def turn(state, answer, incoming, blocks, flipped, group, forward, backward):
     shape = state.shape[1:]
     subs = answer.shape[1]
 
     def kernel(*refs):
         state_in, _, block_ref = refs[:3]
         incoming_ref = None if incoming is None else refs[3]
+        flipped_ref = None if flipped is None else refs[4]
         state_out, answer_out, _, carry = refs[-4:]
         position = lax.axis_index("slab")
         member = lax.rem(position, GROUP)
@@ -439,8 +448,10 @@
                     local = state_in[slot]
                     if value is None:
                         value = local
+                    elif flipped is None:
+                        value = local - row_product(value, block_ref, slot, dot_flipped)
                     else:
-                        value = local - row_product(value, block_ref, slot, dot_flipped)
+                        value = local - row_product(value, flipped_ref, slot, dot)
                     state_out[slot] = value
                 carry[...] = value
             if backward:
@@ -455,7 +466,7 @@
                         value = row_product(value, block_ref, slot, dot)
                 carry[...] = value
 
-    operands = (state, answer, blocks) + (() if incoming is None else (incoming,))
+    operands = (state, answer, blocks) + tuple(x for x in (incoming, flipped) if x is not None)
     return pl.pallas_call(
         kernel,
         out_shape=(
@@ -514,22 +525,27 @@
             lambda slab, sub: (slab + GROUP * steps, sub) if slab // GROUP == source else None,
         )
 
-    incoming = joined = None
+    incoming = joined = flipped = None
     answer = jnp.zeros((GROUP, subs) + state.shape[1:], jnp.float32)
     for group in range(turns):
         last = group == turns - 1
-        state, answer, blocks, carry = turn(state, answer, incoming, blocks, group, True, last)
+        state, answer, blocks, carry = turn(
+            state, answer, incoming, blocks, flipped, group, True, last
+        )
         if not last:
             incoming = hop(carry, group, 1)
+        if not group:
+            state, blocks = lax.optimization_barrier((state, blocks))
+            flipped = flip_blocks(blocks)
     for group in reversed(range(turns - 1)):
         incoming = hop(carry, group + 1, -1)
         if group >= turns - 3:
             carry, eliminated = lax.optimization_barrier((carry, eliminated))
-            late = group == turns - 3
-            chosen = [turns - 2] if late else [g for g in range(turns) if g != turns - 2]
-            joined = joined_blocks(joined, lower, weights, rows, eliminated, chosen)
+            joined = joined_blocks(joined, lower, weights, rows, eliminated, turns)
             state, joined = lax.optimization_barrier((state, joined))
-        state, answer, blocks, carry = turn(state, answer, incoming, blocks, group, False, True)
+        state, answer, blocks, carry = turn(
+            state, answer, incoming, blocks, None, group, False, True
+        )
 
     arrived = exchange(answer.reshape((GROUP * subs,) + answer.shape[2:]))
     interior, solved = finish(arrived, *joined)

time: 112 us -> 107 us (0.955)
  waiting for transfers between devices: 30.2 us -> 27.1 us
  Pallas kernels: 31.3 us -> 30.1 us
    ppermute x13, waiting for transfers between devices: 30.2 us -> 27.1 us  [move(): return lax.ppermute(value, ('slab', 'sub'), pairs)]
    pallas_call x1, Pallas kernels: 4.82 us -> 3.68 us  [finish(): pl.pallas_call(kernel, grid=(count,), out_shape=(jax.ShapeDtypeStruct((co...]
  transfers between devices with their start and end apart: 13 -> 13, of which waited for: 5 -> 5; matrix products, arithmetic and copies ran while one was open for 2% -> 2% of each run, Pallas kernels for 19% -> 20%
where the time goes in v1:
time: 107 us
  blocking collectives  33.3 us (31%)
  Pallas kernels  30.1 us (28%)
  waiting for transfers between devices  27.1 us (25%)
  starting transfers between devices  13.3 us (12%)
  local copies, waits for them, and re-layouts  2.38 us (2%)
    all_to_all x2, blocking collectives, exchange(): lax.all_to_all(value, ('slab', 'sub'), 0, 0, axis_index_groups=groups, ti...  33.3 us
    ppermute x13, waiting for transfers between devices, move(): return lax.ppermute(value, ('slab', 'sub'), pairs)  27.1 us
    ppermute x13, starting transfers between devices, move(): return lax.ppermute(value, ('slab', 'sub'), pairs)  13.3 us
    pallas_call x1, Pallas kernels, separator_part(): pl.pallas_call(kernel, out_shape=(jax.ShapeDtypeStruct((GROUP * subs, 2 *...  10.9 us
    pallas_call x2, Pallas kernels, joined_blocks(): pl.pallas_call(kernel, out_shape=(pltpu.HBM((count, 2, 2, size, inner), j...  10 us
    pallas_call x7, Pallas kernels, turn(): pl.pallas_call(kernel, out_shape=(jax.ShapeDtypeStruct(state.shape, jnp.f...  4.34 us
    pallas_call x1, Pallas kernels, finish(): pl.pallas_call(kernel, grid=(count,), out_shape=(jax.ShapeDtypeStruct((co...  3.68 us
  transfers between devices with their start and end apart: 13, of which 5 were waited for; matrix products, arithmetic and copies ran while one was open for 2% of the time, Pallas kernels for 20%

profile of v1, /device:TPU:0, one launch (start us, length us, event | category | flops | bytes accessed | tf_op | source)
XLA Modules:
  0.0 107.0 jit_solution(3002347320918142468)
XLA Ops:
  1.1 1.1 %constant_dynamic-slice_fusion = f32[320,512]{1,0:T(8,128)S(1)} fusion(f32[1024,512]{1,0:T(8,128)} %bitcast.12, s32[]{:T(128)S(6)} %select_n.3), kind=kLoop, calls=%fused_computation | loop fusion | bytes 1310724 | tf_op jit(solution)/shard_map/dynamic_slice | solution.py:82
  2.3 2.6 %collective-permute-start.1 = (f32[320,512]{1,0:T(8,128)S(1)}, f32[320,512]{1,0:T(8,128)S(1)}, u32[]{:S(2)}, u32[]{:S(2)}) collective-permute-start(f32[320,512]{1,0:T(8,128)S(1)} %constant_dynamic-slice_fusion), channel_id=1, source_target_pairs={{0,4},{1,5},{2,6},{3,7},{4,0},{5,1},{6,2},{7,3},{8,12},{9,13},{10,... | collective-permute-start | bytes 1966088 | tf_op jit(solution)/shard_map/ppermute | solution.py:24
  4.9 1.2 %slice.4 = f32[384,512]{1,0:T(8,128)S(1)} slice(f32[1024,512]{1,0:T(8,128)} %bitcast.13), slice={[640:1024], [0:512]} | slice | bytes 1572864 | tf_op jit(solution)/shard_map/slice | solution.py:87
  6.1 1.9 %collective-permute-start.3 = (f32[384,512]{1,0:T(8,128)S(1)}, f32[384,512]{1,0:T(8,128)S(1)}, u32[]{:S(2)}, u32[]{:S(2)}) collective-permute-start(f32[384,512]{1,0:T(8,128)S(1)} %slice.4), channel_id=1, source_target_pairs={{0,4},{1,5},{2,6},{3,7},{4,0},{5,1},{6,2},{7,3},{8,12},{9,13},{10,... | collective-permute-start | bytes 2359304 | tf_op jit(solution)/shard_map/ppermute | solution.py:24
  8.0 10.9 %separator_part.1 = (f32[8,32,512]{2,1,0:T(8,128)S(1)}, f32[4,256,256]{2,1,0:T(8,128)}) custom-call(f32[4,2,256,128]{3,2,1,0:T(8,128)} %bitcast.25, f32[4,2,256,256]{3,2,1,0:T(8,128)} %bitcast.21, f32[4,2,512,256]{3,2,1,0:T(8,128)} %bitcast.18, s32[4,512]{1,0:T(4,128)} %bitcast.15, f32[2,512,128]{2,1,0:T(8,128)} %bitcast.27, f32[2,512,512]{2,1,0:T(8,128)} %bitcast.24), custom_call_target="tpu_custom_call" | custom-call | flops 40000000000 | bytes 1048576 | tf_op jit(solution)/shard_map/separator_part/pallas_call | solution.py:236
  18.9 1.6 %collective-permute-done.1.refs_2_ = f32[320,512]{1,0:T(8,128)S(1)} collective-permute-done((f32[320,512]{1,0:T(8,128)S(1)}, f32[320,512]{1,0:T(8,128)S(1)}, u32[]{:S(2)}, u32[]{:S(2)}) %collective-permute-start.1) | collective-permute-done | bytes 655392 | tf_op jit(solution)/shard_map/ppermute | solution.py:24
  20.5 1.9 %collective-permute-start.2 = (f32[320,512]{1,0:T(8,128)S(1)}, f32[320,512]{1,0:T(8,128)S(1)}, u32[]{:S(2)}, u32[]{:S(2)}) collective-permute-start(f32[320,512]{1,0:T(8,128)S(1)} %collective-permute-done.1.refs_2_), channel_id=1, source_target_pairs={{0,1},{1,0},{2,3},{3,2},{4,5},{5,4},{6,7},{7,6},{8,9},{9,8},{10,11... | collective-permute-start | bytes 1966088 | tf_op jit(solution)/shard_map/ppermute | solution.py:24
  22.4 20.3 %all_to_all.10.refs_8_ = f32[8,32,512]{2,1,0:T(8,128)S(1)} all-to-all(f32[8,32,512]{2,1,0:T(8,128)S(1)} %get-tuple-element.63), channel_id=1, replica_groups={{0,1,2,3,4,5,6,7},{8,9,10,11,12,13,14,15},{16,17,18,19,20,21,22,23},{24..., dimensions={0} | all-to-all | bytes 1048576 | tf_op jit(solution)/shard_map/all_to_all | solution.py:504
  43.4 2.5 %collective-permute-done.4.refs_5_ = f32[320,512]{1,0:T(8,128)S(1)} collective-permute-done((f32[320,512]{1,0:T(8,128)S(1)}, f32[320,512]{1,0:T(8,128)S(1)}, u32[]{:S(2)}, u32[]{:S(2)}) %collective-permute-start.4) | collective-permute-done | bytes 655392 | tf_op jit(solution)/shard_map/ppermute | solution.py:24
  45.9 0.9 collective-permute-done.5.refs_6_
  46.9 1.2 %split_blocks.1 = (bf16[4,2,1024,512]{3,2,1,0:T(8,128)(2,1)S(1)}, f32[4,32,512]{2,1,0:T(8,128)S(1)}) custom-call(f32[1024,512]{1,0:T(8,128)S(1)} %bitcast.14, f32[1024,512]{1,0:T(8,128)S(1)} %collective-permute-done.refs_1_, f32[320,512]{1,0:T(8,128)S(1)} %collective-permute-done.1.refs_2_, f32[320,512]{1,0:T(8,128)S(1)} %collective-permute-done.2.refs_3_, ...), custom_call_target="tpu_custom_call" | custom-call | tf_op jit(solution)/shard_map/split_blocks/pallas_call | solution.py:131
  48.1 2.1 %sweep_turn.7 = (f32[4,32,512]{2,1,0:T(8,128)S(1)}, f32[4,2,32,512]{3,2,1,0:T(8,128)S(1)}, bf16[4,2,1024,512]{3,2,1,0:T(8,128)(2,1)S(1)}, f32[32,512]{1,0:T(8,128)S(1)}) custom-call(f32[4,32,512]{2,1,0:T(8,128)S(1)} %get-tuple-element.68.refs_0_, ...), custom_call_target="tpu_custom_call", output_to_operand_aliasing={{0}: (0, {}), {1}: (1, {}), {2}: (2, {})} | custom-call | tf_op jit(solution)/shard_map/sweep_turn/pallas_call | solution.py:470
  50.2 1.4 %collective-permute-start.7 = (f32[32,512]{1,0:T(8,128)S(1)}, f32[32,512]{1,0:T(8,128)S(1)}, u32[]{:S(2)}, u32[]{:S(2)}) collective-permute-start(f32[32,512]{1,0:T(8,128)S(1)} %get-tuple-element.75), channel_id=1, source_target_pairs={{0,8},{1,9},{2,10},{3,11},{4,12},{5,13},{6,14},{7,15}} | collective-permute-start | bytes 196616 | tf_op jit(solution)/shard_map/ppermute | solution.py:24
  51.7 1.9 %collective-permute-done.7.refs_3_ = f32[32,512]{1,0:T(8,128)S(1)} collective-permute-done((f32[32,512]{1,0:T(8,128)S(1)}, f32[32,512]{1,0:T(8,128)S(1)}, u32[]{:S(2)}, u32[]{:S(2)}) %collective-permute-start.7) | collective-permute-done | bytes 65568 | tf_op jit(solution)/shard_map/ppermute | solution.py:24
  53.6 0.7 collective-permute-start.8
  54.3 0.7 collective-permute-start.9
  55.2 0.7 collective-permute-start.10
  55.8 9.9 %joined_blocks.2 = (bf16[4,2,2,512,256]{4,3,2,1,0:T(8,128)(2,1)}, f32[4,256,256]{2,1,0:T(8,128)}) custom-call(f32[4,2,256,256]{3,2,1,0:T(8,128)} %bitcast.22, f32[4,2,512,256]{3,2,1,0:T(8,128)} %bitcast.19, s32[4,512]{1,0:T(4,128)S(1)} %bitcast.16, f32[4,256,256]{2,1,0:T(8,128)} %get-tuple-element.95.eliminated_hbm), custom_call_target="tpu_custom_call" | custom-call | flops 1 | bytes 1 | tf_op jit(solution)/shard_map/joined_blocks/pallas_call | solution.py:336
  65.8 0.7 collective-permute-start.11
  66.7 1.6 %collective-permute-start.12 = (f32[32,512]{1,0:T(8,128)S(1)}, f32[32,512]{1,0:T(8,128)S(1)}, u32[]{:S(2)}, u32[]{:S(2)}) collective-permute-start(f32[32,512]{1,0:T(8,128)S(1)} %get-tuple-element.106), channel_id=1, source_target_pairs={{8,0},{9,1},{10,2},{11,3},{12,4},{13,5},{14,6},{15,7}} | collective-permute-start | bytes 196616 | tf_op jit(solution)/shard_map/ppermute | solution.py:24
  68.2 20.1 %collective-permute-done.12.refs_3_ = f32[32,512]{1,0:T(8,128)S(1)} collective-permute-done((f32[32,512]{1,0:T(8,128)S(1)}, f32[32,512]{1,0:T(8,128)S(1)}, u32[]{:S(2)}, u32[]{:S(2)}) %collective-permute-start.12) | collective-permute-done | bytes 65568 | tf_op jit(solution)/shard_map/ppermute | solution.py:24
  88.4 2.0 %sweep_turn.13 = (f32[4,32,512]{2,1,0:T(8,128)S(1)}, f32[4,2,32,512]{3,2,1,0:T(8,128)S(1)}, bf16[4,2,1024,512]{3,2,1,0:T(8,128)(2,1)S(1)}, f32[32,512]{1,0:T(8,128)}) custom-call(f32[4,32,512]{2,1,0:T(8,128)S(1)} %get-tuple-element.103.refs_0_, ...), custom_call_target="tpu_custom_call", output_to_operand_aliasing={{0}: (0, {}), {1}: (1, {}), {2}: (2, {})} | custom-call | tf_op jit(solution)/shard_map/sweep_turn/pallas_call | solution.py:470
  90.3 13.0 %all_to_all.11.arrived_ref = f32[8,32,512]{2,1,0:T(8,128)S(1)} all-to-all(f32[8,32,512]{2,1,0:T(8,128)S(1)} %bitcast.10), channel_id=1, replica_groups={{0,1,2,3,4,5,6,7},{8,9,10,11,12,13,14,15},{16,17,18,19,20,21,22,23},{24..., dimensions={0} | all-to-all | bytes 1048576 | tf_op jit(solution)/shard_map/all_to_all | solution.py:504
  103.3 3.7 %finish.1 = (f32[4,2,256,128]{3,2,1,0:T(8,128)}, f32[2,512,128]{2,1,0:T(8,128)}) custom-call(f32[8,32,512]{2,1,0:T(8,128)S(1)} %all_to_all.11.arrived_ref, bf16[4,2,2,512,256]{4,3,2,1,0:T(8,128)(2,1)S(1)} %copy-done, f32[4,256,256]{2,1,0:T(8,128)S(1)} %copy-done.2), custom_call_target="tpu_custom_call" | custom-call | tf_op jit(solution)/shard_map/finish/pallas_call | solution.py:387
  (28 shorter events, 1.7 us)
Async XLA Ops:
  0.6 5.4 %collective-permute-start = (f32[1024,512]{1,0:T(8,128)}, f32[1024,512]{1,0:T(8,128)S(1)}, u32[]{:S(2)}, u32[]{:S(2)}) collective-permute-start(f32[1024,512]{1,0:T(8,128)} %bitcast.11), channel_id=1, source_target_pairs={{0,2},{1,3},{2,0},{3,1},{4,6},{5,7},{6,4},{7,5},{8,10},{9,11},{10,... | collective-permute-start | bytes 6291464 | tf_op jit(solution)/shard_map/ppermute | solution.py:24
  2.3 18.2 %collective-permute-start.1 = (f32[320,512]{1,0:T(8,128)S(1)}, f32[320,512]{1,0:T(8,128)S(1)}, u32[]{:S(2)}, u32[]{:S(2)}) collective-permute-start(f32[320,512]{1,0:T(8,128)S(1)} %constant_dynamic-slice_fusion), channel_id=1, source_target_pairs={{0,4},{1,5},{2,6},{3,7},{4,0},{5,1},{6,2},{7,3},{8,12},{9,13},{10,... | collective-permute-start | bytes 1966088 | tf_op jit(solution)/shard_map/ppermute | solution.py:24
  6.1 36.6 %collective-permute-start.3 = (f32[384,512]{1,0:T(8,128)S(1)}, f32[384,512]{1,0:T(8,128)S(1)}, u32[]{:S(2)}, u32[]{:S(2)}) collective-permute-start(f32[384,512]{1,0:T(8,128)S(1)} %slice.4), channel_id=1, source_target_pairs={{0,4},{1,5},{2,6},{3,7},{4,0},{5,1},{6,2},{7,3},{8,12},{9,13},{10,... | collective-permute-start | bytes 2359304 | tf_op jit(solution)/shard_map/ppermute | solution.py:24
  8.0 38.8 %copy-start.1 = (f32[1,2,512,512]{3,2,1,0:T(8,128)S(1)}, f32[1,2,512,512]{3,2,1,0:T(8,128)}, u32[]{:S(2)}) copy-start(f32[1,2,512,512]{3,2,1,0:T(8,128)} %param.13) | copy-start | bytes 6291460
  20.5 22.2 %collective-permute-start.2 = (f32[320,512]{1,0:T(8,128)S(1)}, f32[320,512]{1,0:T(8,128)S(1)}, u32[]{:S(2)}, u32[]{:S(2)}) collective-permute-start(f32[320,512]{1,0:T(8,128)S(1)} %collective-permute-done.1.refs_2_), channel_id=1, source_target_pairs={{0,1},{1,0},{2,3},{3,2},{4,5},{5,4},{6,7},{7,6},{8,9},{9,8},{10,11... | collective-permute-start | bytes 1966088 | tf_op jit(solution)/shard_map/ppermute | solution.py:24
  42.7 4.2 %collective-permute-start.6 = (f32[384,512]{1,0:T(8,128)S(1)}, f32[384,512]{1,0:T(8,128)S(1)}, u32[]{:S(2)}, u32[]{:S(2)}) collective-permute-start(f32[384,512]{1,0:T(8,128)S(1)} %collective-permute-done.3.refs_4_), channel_id=1, source_target_pairs={{0,2},{1,3},{2,0},{3,1},{4,6},{5,7},{6,4},{7,5},{8,10},{9,11},{10,... | collective-permute-start | bytes 2359304 | tf_op jit(solution)/shard_map/ppermute | solution.py:24
  42.9 3.1 %collective-permute-start.4 = (f32[320,512]{1,0:T(8,128)S(1)}, f32[320,512]{1,0:T(8,128)S(1)}, u32[]{:S(2)}, u32[]{:S(2)}) collective-permute-start(f32[320,512]{1,0:T(8,128)S(1)} %collective-permute-done.1.refs_2_), channel_id=1, source_target_pairs={{0,2},{1,3},{2,0},{3,1},{4,6},{5,7},{6,4},{7,5},{8,10},{9,11},{10,... | collective-permute-start | bytes 1966088 | tf_op jit(solution)/shard_map/ppermute | solution.py:24
  43.2 3.6 %collective-permute-start.5 = (f32[320,512]{1,0:T(8,128)S(1)}, f32[320,512]{1,0:T(8,128)S(1)}, u32[]{:S(2)}, u32[]{:S(2)}) collective-permute-start(f32[320,512]{1,0:T(8,128)S(1)} %collective-permute-done.2.refs_3_), channel_id=1, source_target_pairs={{0,2},{1,3},{2,0},{3,1},{4,6},{5,7},{6,4},{7,5},{8,10},{9,11},{10,... | collective-permute-start | bytes 1966088 | tf_op jit(solution)/shard_map/ppermute | solution.py:24
  50.2 3.3 %collective-permute-start.7 = (f32[32,512]{1,0:T(8,128)S(1)}, f32[32,512]{1,0:T(8,128)S(1)}, u32[]{:S(2)}, u32[]{:S(2)}) collective-permute-start(f32[32,512]{1,0:T(8,128)S(1)} %get-tuple-element.75), channel_id=1, source_target_pairs={{0,8},{1,9},{2,10},{3,11},{4,12},{5,13},{6,14},{7,15}} | collective-permute-start | bytes 196616 | tf_op jit(solution)/shard_map/ppermute | solution.py:24
  53.6 0.7 collective-permute-start.8
  54.3 0.7 collective-permute-start.9
  54.9 0.9 copy-start.3
  55.2 10.6 %collective-permute-start.10 = (f32[32,512]{1,0:T(8,128)S(1)}, f32[32,512]{1,0:T(8,128)S(1)}, u32[]{:S(2)}, u32[]{:S(2)}) collective-permute-start(f32[32,512]{1,0:T(8,128)S(1)} %get-tuple-element.85), channel_id=1, source_target_pairs={{24,16},{25,17},{26,18},{27,19},{28,20},{29,21},{30,22},{31,23}} | collective-permute-start | bytes 196616 | tf_op jit(solution)/shard_map/ppermute | solution.py:24
  65.8 0.8 collective-permute-start.11
  66.6 36.7 %copy-start = (bf16[4,2,2,512,256]{4,3,2,1,0:T(8,128)(2,1)S(1)}, bf16[4,2,2,512,256]{4,3,2,1,0:T(8,128)(2,1)}, u32[]{:S(2)}) copy-start(bf16[4,2,2,512,256]{4,3,2,1,0:T(8,128)(2,1)} %get-tuple-element.108.joined_ref) | copy-start | bytes 12582916
  66.6 36.7 %copy-start.2 = (f32[4,256,256]{2,1,0:T(8,128)S(1)}, f32[4,256,256]{2,1,0:T(8,128)}, u32[]{:S(2)}) copy-start(f32[4,256,256]{2,1,0:T(8,128)} %get-tuple-element.109.plain_ref) | copy-start | bytes 3145732
  66.7 21.7 %collective-permute-start.12 = (f32[32,512]{1,0:T(8,128)S(1)}, f32[32,512]{1,0:T(8,128)S(1)}, u32[]{:S(2)}, u32[]{:S(2)}) collective-permute-start(f32[32,512]{1,0:T(8,128)S(1)} %get-tuple-element.106), channel_id=1, source_target_pairs={{8,0},{9,1},{10,2},{11,3},{12,4},{13,5},{14,6},{15,7}} | collective-permute-start | bytes 196616 | tf_op jit(solution)/shard_map/ppermute | solution.py:24

commit v2 on v1

--- a/solution.py
+++ b/solution.py
@@ -201,21 +201,25 @@
         rows_copy.wait()
         for b in range(count):
             spread[b] = spread_of(rows_ref[b : b + 1])
-        for b in range(count):
-            for copy in copies(b):
-                copy.wait()
-            if b + AHEAD < count:
-                for copy in copies(b + AHEAD):
-                    copy.start()
-            elif b + AHEAD == count:
+        for pair in range(0, count, 2):
+            now = range(pair, min(pair + 2, count))
+            for b in now:
+                for copy in copies(b):
+                    copy.wait()
+            for b in now:
+                if b + 2 < count:
+                    for copy in copies(b + 2):
+                        copy.start()
+            if pair + 2 >= count:
                 right_copy.start()
                 inverse_copy.start()
-            eliminated = column_product(lower_ref.at[b], side_by_side(load_ref.at[b]))
-            eliminated_ref[b] = eliminated.T
-            leaving(b).start()
-            coupled = column_product(weight_ref.at[b], eliminated)
-            load = spread_product(spread[b], coupled)
-            total[...] = total[...] + load if b else load
+            eliminated = [column_product(lower_ref.at[b], side_by_side(load_ref.at[b])) for b in now]
+            for b, value in zip(now, eliminated):
+                eliminated_ref[b] = value.T
+                leaving(b).start()
+            coupled = [column_product(weight_ref.at[b], value) for b, value in zip(now, eliminated)]
+            load = sum(spread_product(spread[b], value) for b, value in zip(now, coupled))
+            total[...] = total[...] + load if pair else load
 
         right_copy.wait()
         inverse_copy.wait()
@@ -364,42 +368,47 @@
     width = height // 2
     shots = pieces * width
 
-    def kernel(arrived_ref, joined_ref, plain_ref, interior_out, solution_out, solved):
-        block = pl.program_id(0)
-
-        @pl.when(block == 0)
-        def _():
-            for half in range(2):
-                for sub in range(subs):
-                    for member in range(GROUP):
-                        start = half * shots + (sub * GROUP + member) * width
-                        solved[start : start + width] = arrived_ref[
-                            member * subs + sub, half * width : (half + 1) * width
-                        ]
-                solution_out[half] = solved[half * shots : (half + 1) * shots].T
-
+    def kernel(arrived_ref, joined_ref, plain_ref, interior_hbm, solution_hbm, solved, interior, solution, left):
+        for half in range(2):
+            for sub in range(subs):
+                for member in range(GROUP):
+                    start = half * shots + (sub * GROUP + member) * width
+                    solved[start : start + width] = arrived_ref[
+                        member * subs + sub, half * width : (half + 1) * width
+                    ]
         rows_now = split(solved[...])
-        real = near_dot(rows_now, (joined_ref[block, 0, 0], joined_ref[block, 0, 1]))
-        imag = near_dot(rows_now, (joined_ref[block, 1, 0], joined_ref[block, 1, 1]))
-        interior_out[0, 0] = (plain_ref[block, :shots] - (real[:shots] - imag[shots:])).T
-        interior_out[0, 1] = (plain_ref[block, shots:] - (real[shots:] + imag[:shots])).T
-
+        for half in range(2):
+            solution[half] = solved[half * shots : (half + 1) * shots].T
+        copies = [pltpu.make_async_copy(solution, solution_hbm, left.at[count])]
+        copies[0].start()
+        for block in range(count):
+            real = near_dot(rows_now, (joined_ref[block, 0, 0], joined_ref[block, 0, 1]))
+            imag = near_dot(rows_now, (joined_ref[block, 1, 0], joined_ref[block, 1, 1]))
+            interior[block, 0] = (plain_ref[block, :shots] - (real[:shots] - imag[shots:])).T
+            interior[block, 1] = (plain_ref[block, shots:] - (real[shots:] + imag[:shots])).T
+            copies.append(
+                pltpu.make_async_copy(interior.at[block], interior_hbm.at[block], left.at[block])
+            )
+            copies[-1].start()
+        for copy in copies:
+            copy.wait()
+
+    hbm = pl.BlockSpec(memory_space=pltpu.HBM)
     return pl.pallas_call(
         kernel,
-        grid=(count,),
         out_shape=(
-            jax.ShapeDtypeStruct((count, 2, inner, shots), jnp.float32),
-            jax.ShapeDtypeStruct((2, size, shots), jnp.float32),
+            pltpu.HBM((count, 2, inner, shots), jnp.float32),
+            pltpu.HBM((2, size, shots), jnp.float32),
         ),
         in_specs=[whole()] * 3,
-        out_specs=(
-            pl.BlockSpec((1, 2, inner, shots), lambda b: (b, 0, 0, 0)),
-            pl.BlockSpec((2, size, shots), lambda b: (0, 0, 0)),
-        ),
+        out_specs=(hbm, hbm),
         scratch_shapes=[
             pltpu.VMEM((2 * shots, size), jnp.float32),
+            pltpu.VMEM((count, 2, inner, shots), jnp.float32),
+            pltpu.VMEM((2, size, shots), jnp.float32),
+            pltpu.SemaphoreType.DMA((count + 1,)),
         ],
-        compiler_params=pltpu.CompilerParams(vmem_limit_bytes=16 * MIB),
+        compiler_params=pltpu.CompilerParams(vmem_limit_bytes=12 * MIB),
         name="finish",
     )(arrived, joined, plain)
 

time: 107 us -> 107 us (level)
  Pallas kernels: 30.1 us -> 27.7 us
  waiting for transfers between devices: 27.1 us -> 28.6 us
    pallas_call x1, Pallas kernels: 10.9 us -> 9.35 us  [separator_part(): pl.pallas_call(kernel, out_shape=(jax.ShapeDtypeStruct((GROUP * subs, 2 *...]
    ppermute x13, waiting for transfers between devices: 27.1 us -> 28.6 us  [move(): return lax.ppermute(value, ('slab', 'sub'), pairs)]
  transfers between devices with their start and end apart: 13 -> 13, of which waited for: 5 -> 5; matrix products, arithmetic and copies ran while one was open for 2% -> 2% of each run, Pallas kernels for 20% -> 18%
where the time goes in v2:
time: 107 us; the launch traced here: 106 us
  blocking collectives  33.3 us (31%)
  waiting for transfers between devices  28.6 us (27%)
  Pallas kernels  27.7 us (26%)
  starting transfers between devices  13.3 us (12%)
  local copies, waits for them, and re-layouts  2.38 us (2%)
    all_to_all x2, blocking collectives, exchange(): lax.all_to_all(value, ('slab', 'sub'), 0, 0, axis_index_groups=groups, ti...  33.3 us
    ppermute x13, waiting for transfers between devices, move(): return lax.ppermute(value, ('slab', 'sub'), pairs)  28.6 us
    ppermute x13, starting transfers between devices, move(): return lax.ppermute(value, ('slab', 'sub'), pairs)  13.3 us
    pallas_call x2, Pallas kernels, joined_blocks(): pl.pallas_call(kernel, out_shape=(pltpu.HBM((count, 2, 2, size, inner), j...  10 us
    pallas_call x1, Pallas kernels, separator_part(): pl.pallas_call(kernel, out_shape=(jax.ShapeDtypeStruct((GROUP * subs, 2 *...  9.35 us
    pallas_call x7, Pallas kernels, turn(): pl.pallas_call(kernel, out_shape=(jax.ShapeDtypeStruct(state.shape, jnp.f...  4.34 us
    pallas_call x1, Pallas kernels, finish(): pl.pallas_call(kernel, out_shape=(pltpu.HBM((count, 2, inner, shots), jnp...  2.76 us
  transfers between devices with their start and end apart: 13, of which 5 were waited for; matrix products, arithmetic and copies ran while one was open for 2% of the time, Pallas kernels for 18%

profile of v2, /device:TPU:0, one launch (start us, length us, event | category | flops | bytes accessed | tf_op | source)
XLA Modules:
  0.0 106.3 jit_solution(3811732185767885734)
XLA Ops:
  1.1 1.1 %constant_dynamic-slice_fusion = f32[320,512]{1,0:T(8,128)S(1)} fusion(f32[1024,512]{1,0:T(8,128)} %bitcast.12, s32[]{:T(128)S(6)} %select_n.3), kind=kLoop, calls=%fused_computation | loop fusion | bytes 1310724 | tf_op jit(solution)/shard_map/dynamic_slice | solution.py:82
  2.3 2.6 %collective-permute-start.1 = (f32[320,512]{1,0:T(8,128)S(1)}, f32[320,512]{1,0:T(8,128)S(1)}, u32[]{:S(2)}, u32[]{:S(2)}) collective-permute-start(f32[320,512]{1,0:T(8,128)S(1)} %constant_dynamic-slice_fusion), channel_id=1, source_target_pairs={{0,4},{1,5},{2,6},{3,7},{4,0},{5,1},{6,2},{7,3},{8,12},{9,13},{10,... | collective-permute-start | bytes 1966088 | tf_op jit(solution)/shard_map/ppermute | solution.py:24
  4.9 1.2 %slice.4 = f32[384,512]{1,0:T(8,128)S(1)} slice(f32[1024,512]{1,0:T(8,128)} %bitcast.13), slice={[640:1024], [0:512]} | slice | bytes 1572864 | tf_op jit(solution)/shard_map/slice | solution.py:87
  6.1 1.9 %collective-permute-start.3 = (f32[384,512]{1,0:T(8,128)S(1)}, f32[384,512]{1,0:T(8,128)S(1)}, u32[]{:S(2)}, u32[]{:S(2)}) collective-permute-start(f32[384,512]{1,0:T(8,128)S(1)} %slice.4), channel_id=1, source_target_pairs={{0,4},{1,5},{2,6},{3,7},{4,0},{5,1},{6,2},{7,3},{8,12},{9,13},{10,... | collective-permute-start | bytes 2359304 | tf_op jit(solution)/shard_map/ppermute | solution.py:24
  8.0 9.4 %separator_part.1 = (f32[8,32,512]{2,1,0:T(8,128)S(1)}, f32[4,256,256]{2,1,0:T(8,128)}) custom-call(f32[4,2,256,128]{3,2,1,0:T(8,128)} %bitcast.25, f32[4,2,256,256]{3,2,1,0:T(8,128)} %bitcast.21, f32[4,2,512,256]{3,2,1,0:T(8,128)} %bitcast.18, s32[4,512]{1,0:T(4,128)} %bitcast.15, f32[2,512,128]{2,1,0:T(8,128)} %bitcast.27, f32[2,512,512]{2,1,0:T(8,128)} %bitcast.24), custom_call_target="tpu_custom_call" | custom-call | flops 40000000000 | bytes 1048576 | tf_op jit(solution)/shard_map/separator_part/pallas_call | solution.py:240
  17.4 3.1 %collective-permute-done.1.refs_2_ = f32[320,512]{1,0:T(8,128)S(1)} collective-permute-done((f32[320,512]{1,0:T(8,128)S(1)}, f32[320,512]{1,0:T(8,128)S(1)}, u32[]{:S(2)}, u32[]{:S(2)}) %collective-permute-start.1) | collective-permute-done | bytes 655392 | tf_op jit(solution)/shard_map/ppermute | solution.py:24
  20.5 1.9 %collective-permute-start.2 = (f32[320,512]{1,0:T(8,128)S(1)}, f32[320,512]{1,0:T(8,128)S(1)}, u32[]{:S(2)}, u32[]{:S(2)}) collective-permute-start(f32[320,512]{1,0:T(8,128)S(1)} %collective-permute-done.1.refs_2_), channel_id=1, source_target_pairs={{0,1},{1,0},{2,3},{3,2},{4,5},{5,4},{6,7},{7,6},{8,9},{9,8},{10,11... | collective-permute-start | bytes 1966088 | tf_op jit(solution)/shard_map/ppermute | solution.py:24
  22.4 20.3 %all_to_all.10.refs_8_ = f32[8,32,512]{2,1,0:T(8,128)S(1)} all-to-all(f32[8,32,512]{2,1,0:T(8,128)S(1)} %get-tuple-element.63), channel_id=1, replica_groups={{0,1,2,3,4,5,6,7},{8,9,10,11,12,13,14,15},{16,17,18,19,20,21,22,23},{24..., dimensions={0} | all-to-all | bytes 1048576 | tf_op jit(solution)/shard_map/all_to_all | solution.py:513
  43.4 2.5 %collective-permute-done.4.refs_5_ = f32[320,512]{1,0:T(8,128)S(1)} collective-permute-done((f32[320,512]{1,0:T(8,128)S(1)}, f32[320,512]{1,0:T(8,128)S(1)}, u32[]{:S(2)}, u32[]{:S(2)}) %collective-permute-start.4) | collective-permute-done | bytes 655392 | tf_op jit(solution)/shard_map/ppermute | solution.py:24
  45.9 0.9 collective-permute-done.5.refs_6_
  46.9 1.2 %split_blocks.1 = (bf16[4,2,1024,512]{3,2,1,0:T(8,128)(2,1)S(1)}, f32[4,32,512]{2,1,0:T(8,128)S(1)}) custom-call(f32[1024,512]{1,0:T(8,128)S(1)} %bitcast.14, f32[1024,512]{1,0:T(8,128)S(1)} %collective-permute-done.refs_1_, f32[320,512]{1,0:T(8,128)S(1)} %collective-permute-done.1.refs_2_, f32[320,512]{1,0:T(8,128)S(1)} %collective-permute-done.2.refs_3_, ...), custom_call_target="tpu_custom_call" | custom-call | tf_op jit(solution)/shard_map/split_blocks/pallas_call | solution.py:131
  48.1 2.1 %sweep_turn.7 = (f32[4,32,512]{2,1,0:T(8,128)S(1)}, f32[4,2,32,512]{3,2,1,0:T(8,128)S(1)}, bf16[4,2,1024,512]{3,2,1,0:T(8,128)(2,1)S(1)}, f32[32,512]{1,0:T(8,128)S(1)}) custom-call(f32[4,32,512]{2,1,0:T(8,128)S(1)} %get-tuple-element.68.refs_0_, ...), custom_call_target="tpu_custom_call", output_to_operand_aliasing={{0}: (0, {}), {1}: (1, {}), {2}: (2, {})} | custom-call | tf_op jit(solution)/shard_map/sweep_turn/pallas_call | solution.py:479
  50.2 1.4 %collective-permute-start.7 = (f32[32,512]{1,0:T(8,128)S(1)}, f32[32,512]{1,0:T(8,128)S(1)}, u32[]{:S(2)}, u32[]{:S(2)}) collective-permute-start(f32[32,512]{1,0:T(8,128)S(1)} %get-tuple-element.75), channel_id=1, source_target_pairs={{0,8},{1,9},{2,10},{3,11},{4,12},{5,13},{6,14},{7,15}} | collective-permute-start | bytes 196616 | tf_op jit(solution)/shard_map/ppermute | solution.py:24
  51.7 1.9 %collective-permute-done.7.refs_3_ = f32[32,512]{1,0:T(8,128)S(1)} collective-permute-done((f32[32,512]{1,0:T(8,128)S(1)}, f32[32,512]{1,0:T(8,128)S(1)}, u32[]{:S(2)}, u32[]{:S(2)}) %collective-permute-start.7) | collective-permute-done | bytes 65568 | tf_op jit(solution)/shard_map/ppermute | solution.py:24
  53.6 0.7 collective-permute-start.8
  54.3 0.7 collective-permute-start.9
  55.2 0.7 collective-permute-start.10
  55.8 9.9 %joined_blocks.2 = (bf16[4,2,2,512,256]{4,3,2,1,0:T(8,128)(2,1)}, f32[4,256,256]{2,1,0:T(8,128)}) custom-call(f32[4,2,256,256]{3,2,1,0:T(8,128)} %bitcast.22, f32[4,2,512,256]{3,2,1,0:T(8,128)} %bitcast.19, s32[4,512]{1,0:T(4,128)S(1)} %bitcast.16, f32[4,256,256]{2,1,0:T(8,128)} %get-tuple-element.95.eliminated_hbm), custom_call_target="tpu_custom_call" | custom-call | flops 1 | bytes 1 | tf_op jit(solution)/shard_map/joined_blocks/pallas_call | solution.py:340
  65.8 0.7 collective-permute-start.11
  66.7 1.6 %collective-permute-start.12 = (f32[32,512]{1,0:T(8,128)S(1)}, f32[32,512]{1,0:T(8,128)S(1)}, u32[]{:S(2)}, u32[]{:S(2)}) collective-permute-start(f32[32,512]{1,0:T(8,128)S(1)} %get-tuple-element.106), channel_id=1, source_target_pairs={{8,0},{9,1},{10,2},{11,3},{12,4},{13,5},{14,6},{15,7}} | collective-permute-start | bytes 196616 | tf_op jit(solution)/shard_map/ppermute | solution.py:24
  68.2 20.1 %collective-permute-done.12.refs_3_ = f32[32,512]{1,0:T(8,128)S(1)} collective-permute-done((f32[32,512]{1,0:T(8,128)S(1)}, f32[32,512]{1,0:T(8,128)S(1)}, u32[]{:S(2)}, u32[]{:S(2)}) %collective-permute-start.12) | collective-permute-done | bytes 65568 | tf_op jit(solution)/shard_map/ppermute | solution.py:24
  88.4 2.0 %sweep_turn.13 = (f32[4,32,512]{2,1,0:T(8,128)S(1)}, f32[4,2,32,512]{3,2,1,0:T(8,128)S(1)}, bf16[4,2,1024,512]{3,2,1,0:T(8,128)(2,1)S(1)}, f32[32,512]{1,0:T(8,128)}) custom-call(f32[4,32,512]{2,1,0:T(8,128)S(1)} %get-tuple-element.103.refs_0_, ...), custom_call_target="tpu_custom_call", output_to_operand_aliasing={{0}: (0, {}), {1}: (1, {}), {2}: (2, {})} | custom-call | tf_op jit(solution)/shard_map/sweep_turn/pallas_call | solution.py:479
  90.3 13.0 %all_to_all.11.arrived_ref = f32[8,32,512]{2,1,0:T(8,128)S(1)} all-to-all(f32[8,32,512]{2,1,0:T(8,128)S(1)} %bitcast.10), channel_id=1, replica_groups={{0,1,2,3,4,5,6,7},{8,9,10,11,12,13,14,15},{16,17,18,19,20,21,22,23},{24..., dimensions={0} | all-to-all | bytes 1048576 | tf_op jit(solution)/shard_map/all_to_all | solution.py:513
  103.3 2.8 %finish.1 = (f32[4,2,256,128]{3,2,1,0:T(8,128)}, f32[2,512,128]{2,1,0:T(8,128)}) custom-call(f32[8,32,512]{2,1,0:T(8,128)S(1)} %all_to_all.11.arrived_ref, bf16[4,2,2,512,256]{4,3,2,1,0:T(8,128)(2,1)S(1)} %copy-done, f32[4,256,256]{2,1,0:T(8,128)S(1)} %copy-done.2), custom_call_target="tpu_custom_call" | custom-call | tf_op jit(solution)/shard_map/finish/pallas_call | solution.py:397
  (28 shorter events, 1.7 us)
Async XLA Ops:
  0.6 5.4 %collective-permute-start = (f32[1024,512]{1,0:T(8,128)}, f32[1024,512]{1,0:T(8,128)S(1)}, u32[]{:S(2)}, u32[]{:S(2)}) collective-permute-start(f32[1024,512]{1,0:T(8,128)} %bitcast.11), channel_id=1, source_target_pairs={{0,2},{1,3},{2,0},{3,1},{4,6},{5,7},{6,4},{7,5},{8,10},{9,11},{10,... | collective-permute-start | bytes 6291464 | tf_op jit(solution)/shard_map/ppermute | solution.py:24
  2.3 18.2 %collective-permute-start.1 = (f32[320,512]{1,0:T(8,128)S(1)}, f32[320,512]{1,0:T(8,128)S(1)}, u32[]{:S(2)}, u32[]{:S(2)}) collective-permute-start(f32[320,512]{1,0:T(8,128)S(1)} %constant_dynamic-slice_fusion), channel_id=1, source_target_pairs={{0,4},{1,5},{2,6},{3,7},{4,0},{5,1},{6,2},{7,3},{8,12},{9,13},{10,... | collective-permute-start | bytes 1966088 | tf_op jit(solution)/shard_map/ppermute | solution.py:24
  6.1 36.6 %collective-permute-start.3 = (f32[384,512]{1,0:T(8,128)S(1)}, f32[384,512]{1,0:T(8,128)S(1)}, u32[]{:S(2)}, u32[]{:S(2)}) collective-permute-start(f32[384,512]{1,0:T(8,128)S(1)} %slice.4), channel_id=1, source_target_pairs={{0,4},{1,5},{2,6},{3,7},{4,0},{5,1},{6,2},{7,3},{8,12},{9,13},{10,... | collective-permute-start | bytes 2359304 | tf_op jit(solution)/shard_map/ppermute | solution.py:24
  8.0 38.8 %copy-start.1 = (f32[1,2,512,512]{3,2,1,0:T(8,128)S(1)}, f32[1,2,512,512]{3,2,1,0:T(8,128)}, u32[]{:S(2)}) copy-start(f32[1,2,512,512]{3,2,1,0:T(8,128)} %param.13) | copy-start | bytes 6291460
  20.5 22.2 %collective-permute-start.2 = (f32[320,512]{1,0:T(8,128)S(1)}, f32[320,512]{1,0:T(8,128)S(1)}, u32[]{:S(2)}, u32[]{:S(2)}) collective-permute-start(f32[320,512]{1,0:T(8,128)S(1)} %collective-permute-done.1.refs_2_), channel_id=1, source_target_pairs={{0,1},{1,0},{2,3},{3,2},{4,5},{5,4},{6,7},{7,6},{8,9},{9,8},{10,11... | collective-permute-start | bytes 1966088 | tf_op jit(solution)/shard_map/ppermute | solution.py:24
  42.7 4.2 %collective-permute-start.6 = (f32[384,512]{1,0:T(8,128)S(1)}, f32[384,512]{1,0:T(8,128)S(1)}, u32[]{:S(2)}, u32[]{:S(2)}) collective-permute-start(f32[384,512]{1,0:T(8,128)S(1)} %collective-permute-done.3.refs_4_), channel_id=1, source_target_pairs={{0,2},{1,3},{2,0},{3,1},{4,6},{5,7},{6,4},{7,5},{8,10},{9,11},{10,... | collective-permute-start | bytes 2359304 | tf_op jit(solution)/shard_map/ppermute | solution.py:24
  42.9 3.1 %collective-permute-start.4 = (f32[320,512]{1,0:T(8,128)S(1)}, f32[320,512]{1,0:T(8,128)S(1)}, u32[]{:S(2)}, u32[]{:S(2)}) collective-permute-start(f32[320,512]{1,0:T(8,128)S(1)} %collective-permute-done.1.refs_2_), channel_id=1, source_target_pairs={{0,2},{1,3},{2,0},{3,1},{4,6},{5,7},{6,4},{7,5},{8,10},{9,11},{10,... | collective-permute-start | bytes 1966088 | tf_op jit(solution)/shard_map/ppermute | solution.py:24
  43.2 3.6 %collective-permute-start.5 = (f32[320,512]{1,0:T(8,128)S(1)}, f32[320,512]{1,0:T(8,128)S(1)}, u32[]{:S(2)}, u32[]{:S(2)}) collective-permute-start(f32[320,512]{1,0:T(8,128)S(1)} %collective-permute-done.2.refs_3_), channel_id=1, source_target_pairs={{0,2},{1,3},{2,0},{3,1},{4,6},{5,7},{6,4},{7,5},{8,10},{9,11},{10,... | collective-permute-start | bytes 1966088 | tf_op jit(solution)/shard_map/ppermute | solution.py:24
  50.2 3.3 %collective-permute-start.7 = (f32[32,512]{1,0:T(8,128)S(1)}, f32[32,512]{1,0:T(8,128)S(1)}, u32[]{:S(2)}, u32[]{:S(2)}) collective-permute-start(f32[32,512]{1,0:T(8,128)S(1)} %get-tuple-element.75), channel_id=1, source_target_pairs={{0,8},{1,9},{2,10},{3,11},{4,12},{5,13},{6,14},{7,15}} | collective-permute-start | bytes 196616 | tf_op jit(solution)/shard_map/ppermute | solution.py:24
  53.6 0.7 collective-permute-start.8
  54.3 0.7 collective-permute-start.9
  54.9 0.9 copy-start.3
  55.2 10.6 %collective-permute-start.10 = (f32[32,512]{1,0:T(8,128)S(1)}, f32[32,512]{1,0:T(8,128)S(1)}, u32[]{:S(2)}, u32[]{:S(2)}) collective-permute-start(f32[32,512]{1,0:T(8,128)S(1)} %get-tuple-element.85), channel_id=1, source_target_pairs={{24,16},{25,17},{26,18},{27,19},{28,20},{29,21},{30,22},{31,23}} | collective-permute-start | bytes 196616 | tf_op jit(solution)/shard_map/ppermute | solution.py:24
  65.8 0.8 collective-permute-start.11
  66.6 36.7 %copy-start = (bf16[4,2,2,512,256]{4,3,2,1,0:T(8,128)(2,1)S(1)}, bf16[4,2,2,512,256]{4,3,2,1,0:T(8,128)(2,1)}, u32[]{:S(2)}) copy-start(bf16[4,2,2,512,256]{4,3,2,1,0:T(8,128)(2,1)} %get-tuple-element.108.joined_ref) | copy-start | bytes 12582916
  66.6 36.7 %copy-start.2 = (f32[4,256,256]{2,1,0:T(8,128)S(1)}, f32[4,256,256]{2,1,0:T(8,128)}, u32[]{:S(2)}) copy-start(f32[4,256,256]{2,1,0:T(8,128)} %get-tuple-element.109.plain_ref) | copy-start | bytes 3145732
  66.7 21.7 %collective-permute-start.12 = (f32[32,512]{1,0:T(8,128)S(1)}, f32[32,512]{1,0:T(8,128)S(1)}, u32[]{:S(2)}, u32[]{:S(2)}) collective-permute-start(f32[32,512]{1,0:T(8,128)S(1)} %get-tuple-element.106), channel_id=1, source_target_pairs={{8,0},{9,1},{10,2},{11,3},{12,4},{13,5},{14,6},{15,7}} | collective-permute-start | bytes 196616 | tf_op jit(solution)/shard_map/ppermute | solution.py:24

commit v3 on v2

--- a/solution.py
+++ b/solution.py
@@ -11,6 +11,7 @@
 AHEAD = 2
 MIB = 1 << 20
 LIGHT = pl.CostEstimate(flops=1, bytes_accessed=1, transcendentals=0)
+HEAVY = pl.CostEstimate(flops=10**9, bytes_accessed=1 << 24, transcendentals=0)
 
 
 def move(value, target):
@@ -99,34 +100,35 @@
     return pltpu.with_memory_space_constraint(value, pltpu.HBM)
 
 
-def split_blocks(own, near, pieces, far, terms):
+def places(pieces, size):
+    subs = lax.axis_size("sub")
+    here = lax.axis_index("sub")
+    step, direct = plan(size, subs)
+    for c, k, _ in pieces:
+        if c < RELAYED:
+            start = (c * subs + lax.rem(here - k + subs, subs)) * step
+            yield pl.ds(pl.multiple_of(start, step), step)
+        else:
+            yield pl.ds(RELAYED * subs * step + (c - RELAYED) * direct, direct)
+
+
+def split_blocks(own, near, pieces, terms):
     subs = lax.axis_size("sub")
     size = own.shape[1]
-    step, direct = plan(size, subs)
-    values = [own, near] + [piece for _, _, piece in pieces] + list(far)
-    count = len(pieces)
+    values = [own, near] + [piece for _, _, piece in pieces]
 
     def kernel(*refs):
-        sources, (terms_ref, out, state) = refs[: len(values)], refs[len(values) : len(values) + 3]
-        here = lax.axis_index("sub")
+        sources, (terms_ref, out, state) = refs[: len(values)], refs[len(values) :]
         member = lax.rem(lax.axis_index("slab"), GROUP)
         for slot in range(GROUP):
             value = terms_ref[(member ^ slot) * subs]
             for sub in range(1, subs):
                 value = value + terms_ref[(member ^ slot) * subs + sub]
             state[slot] = value
-        for i, source in enumerate(sources):
-            if i < 2:
-                out[i, 0], out[i, 1] = split(source[...])
-                continue
-            slot, (c, k, _) = 2 + (i - 2) // count, pieces[(i - 2) % count]
-            if c < RELAYED:
-                start = pl.multiple_of((c * subs + lax.rem(here - k + subs, subs)) * step, step)
-                rows = pl.ds(start, step)
-            else:
-                start = RELAYED * subs * step + (c - RELAYED) * direct
-                rows = pl.ds(start, direct)
-            out[slot, 0, rows], out[slot, 1, rows] = split(source[...])
+        for slot in range(2):
+            out[slot, 0], out[slot, 1] = split(sources[slot][...])
+        for rows, source in zip(places(pieces, size), sources[2:]):
+            out[2, 0, rows], out[2, 1, rows] = split(source[...])
 
     return pl.pallas_call(
         kernel,
@@ -137,8 +139,26 @@
         in_specs=[whole()] * (len(values) + 1),
         out_specs=(whole(), whole()),
         compiler_params=pltpu.CompilerParams(vmem_limit_bytes=16 * MIB),
+        cost_estimate=HEAVY,
         name="split_blocks",
     )(*values, terms)
+
+
+def split_last(blocks, pieces, far):
+    def kernel(_, *refs):
+        out = refs[-1]
+        for rows, source in zip(places(pieces, blocks.shape[-1]), refs[:-1]):
+            out[3, 0, rows], out[3, 1, rows] = split(source[...])
+
+    return pl.pallas_call(
+        kernel,
+        out_shape=pltpu.VMEM(blocks.shape, blocks.dtype),
+        in_specs=[whole()] * (1 + len(far)),
+        out_specs=whole(),
+        input_output_aliases={0: 0},
+        compiler_params=pltpu.CompilerParams(vmem_limit_bytes=16 * MIB),
+        name="split_last",
+    )(blocks, *far)
 
 
 def near_dot(left, right):
@@ -526,7 +546,8 @@
     settled, terms = lax.optimization_barrier(([piece for _, _, piece in pieces], terms))
     pieces = [(c, k, piece) for (c, k, _), piece in zip(pieces, settled)]
     far = [swap(piece, 1) if sent is None else sent for piece, sent in zip(settled, early)]
-    blocks, state = split_blocks(own, near, pieces, far, terms)
+    blocks, state = split_blocks(own, near, pieces, terms)
+    blocks = split_last(blocks, pieces, far)
 
     def hop(value, source, steps):
         return move(

time: 107 us -> 106 us (level)
  transfers between devices with their start and end apart: 13 -> 13, of which waited for: 5 -> 5; matrix products, arithmetic and copies ran while one was open for 2% -> 2% of each run, Pallas kernels for 18% -> 19%
where the time goes in v3:
time: 106 us; the launch traced here: 105 us
  blocking collectives  33.3 us (31%)
  Pallas kernels  27.7 us (26%)
  waiting for transfers between devices  27.6 us (26%)
  starting transfers between devices  13.3 us (13%)
  local copies, waits for them, and re-layouts  2.38 us (2%)
    all_to_all x2, blocking collectives, exchange(): lax.all_to_all(value, ('slab', 'sub'), 0, 0, axis_index_groups=groups, ti...  33.3 us
    ppermute x13, waiting for transfers between devices, move(): return lax.ppermute(value, ('slab', 'sub'), pairs)  27.6 us
    ppermute x13, starting transfers between devices, move(): return lax.ppermute(value, ('slab', 'sub'), pairs)  13.3 us
    pallas_call x2, Pallas kernels, joined_blocks(): pl.pallas_call(kernel, out_shape=(pltpu.HBM((count, 2, 2, size, inner), j...  10 us
    pallas_call x1, Pallas kernels, separator_part(): pl.pallas_call(kernel, out_shape=(jax.ShapeDtypeStruct((GROUP * subs, 2 *...  9.35 us
    pallas_call x7, Pallas kernels, turn(): pl.pallas_call(kernel, out_shape=(jax.ShapeDtypeStruct(state.shape, jnp.f...  4.35 us
    pallas_call x1, Pallas kernels, finish(): pl.pallas_call(kernel, out_shape=(pltpu.HBM((count, 2, inner, shots), jnp...  2.76 us
  transfers between devices with their start and end apart: 13, of which 5 were waited for; matrix products, arithmetic and copies ran while one was open for 2% of the time, Pallas kernels for 19%

profile of v3, /device:TPU:0, one launch (start us, length us, event | category | flops | bytes accessed | tf_op | source)
XLA Modules:
  0.0 105.4 jit_solution(2610040631767114448)
XLA Ops:
  1.1 1.1 %constant_dynamic-slice_fusion = f32[320,512]{1,0:T(8,128)S(1)} fusion(f32[1024,512]{1,0:T(8,128)} %bitcast.12, s32[]{:T(128)S(6)} %select_n.3), kind=kLoop, calls=%fused_computation | loop fusion | bytes 1310724 | tf_op jit(solution)/shard_map/dynamic_slice | solution.py:83
  2.3 2.6 %collective-permute-start.1 = (f32[320,512]{1,0:T(8,128)S(1)}, f32[320,512]{1,0:T(8,128)S(1)}, u32[]{:S(2)}, u32[]{:S(2)}) collective-permute-start(f32[320,512]{1,0:T(8,128)S(1)} %constant_dynamic-slice_fusion), channel_id=1, source_target_pairs={{0,4},{1,5},{2,6},{3,7},{4,0},{5,1},{6,2},{7,3},{8,12},{9,13},{10,... | collective-permute-start | bytes 1966088 | tf_op jit(solution)/shard_map/ppermute | solution.py:25
  4.9 1.2 %slice.4 = f32[384,512]{1,0:T(8,128)S(1)} slice(f32[1024,512]{1,0:T(8,128)} %bitcast.13), slice={[640:1024], [0:512]} | slice | bytes 1572864 | tf_op jit(solution)/shard_map/slice | solution.py:88
  6.1 1.9 %collective-permute-start.3 = (f32[384,512]{1,0:T(8,128)S(1)}, f32[384,512]{1,0:T(8,128)S(1)}, u32[]{:S(2)}, u32[]{:S(2)}) collective-permute-start(f32[384,512]{1,0:T(8,128)S(1)} %slice.4), channel_id=1, source_target_pairs={{0,4},{1,5},{2,6},{3,7},{4,0},{5,1},{6,2},{7,3},{8,12},{9,13},{10,... | collective-permute-start | bytes 2359304 | tf_op jit(solution)/shard_map/ppermute | solution.py:25
  8.0 9.4 %separator_part.1 = (f32[8,32,512]{2,1,0:T(8,128)S(1)}, f32[4,256,256]{2,1,0:T(8,128)}) custom-call(f32[4,2,256,128]{3,2,1,0:T(8,128)} %bitcast.25, f32[4,2,256,256]{3,2,1,0:T(8,128)} %bitcast.21, f32[4,2,512,256]{3,2,1,0:T(8,128)} %bitcast.18, s32[4,512]{1,0:T(4,128)} %bitcast.15, f32[2,512,128]{2,1,0:T(8,128)} %bitcast.27, f32[2,512,512]{2,1,0:T(8,128)} %bitcast.24), custom_call_target="tpu_custom_call" | custom-call | flops 40000000000 | bytes 1048576 | tf_op jit(solution)/shard_map/separator_part/pallas_call | solution.py:260
  17.4 3.1 %collective-permute-done.1.refs_2_ = f32[320,512]{1,0:T(8,128)S(1)} collective-permute-done((f32[320,512]{1,0:T(8,128)S(1)}, f32[320,512]{1,0:T(8,128)S(1)}, u32[]{:S(2)}, u32[]{:S(2)}) %collective-permute-start.1) | collective-permute-done | bytes 655392 | tf_op jit(solution)/shard_map/ppermute | solution.py:25
  20.5 1.9 %collective-permute-start.2 = (f32[320,512]{1,0:T(8,128)S(1)}, f32[320,512]{1,0:T(8,128)S(1)}, u32[]{:S(2)}, u32[]{:S(2)}) collective-permute-start(f32[320,512]{1,0:T(8,128)S(1)} %collective-permute-done.1.refs_2_), channel_id=1, source_target_pairs={{0,1},{1,0},{2,3},{3,2},{4,5},{5,4},{6,7},{7,6},{8,9},{9,8},{10,11... | collective-permute-start | bytes 1966088 | tf_op jit(solution)/shard_map/ppermute | solution.py:25
  22.4 20.3 %all_to_all.10.refs_5_ = f32[8,32,512]{2,1,0:T(8,128)S(1)} all-to-all(f32[8,32,512]{2,1,0:T(8,128)S(1)} %get-tuple-element.63), channel_id=1, replica_groups={{0,1,2,3,4,5,6,7},{8,9,10,11,12,13,14,15},{16,17,18,19,20,21,22,23},{24..., dimensions={0} | all-to-all | bytes 1048576 | tf_op jit(solution)/shard_map/all_to_all | solution.py:533
  43.4 0.9 split_blocks.1
  44.3 1.6 %collective-permute-done.4.refs_0_ = f32[320,512]{1,0:T(8,128)S(1)} collective-permute-done((f32[320,512]{1,0:T(8,128)S(1)}, f32[320,512]{1,0:T(8,128)S(1)}, u32[]{:S(2)}, u32[]{:S(2)}) %collective-permute-start.4) | collective-permute-done | bytes 655392 | tf_op jit(solution)/shard_map/ppermute | solution.py:25
  45.9 0.9 collective-permute-done.5.refs_1_
  47.2 2.1 %sweep_turn.7 = (f32[4,32,512]{2,1,0:T(8,128)S(1)}, f32[4,2,32,512]{3,2,1,0:T(8,128)S(1)}, bf16[4,2,1024,512]{3,2,1,0:T(8,128)(2,1)S(1)}, f32[32,512]{1,0:T(8,128)S(1)}) custom-call(f32[4,32,512]{2,1,0:T(8,128)S(1)} %get-tuple-element.68.refs_0_, ...), custom_call_target="tpu_custom_call", output_to_operand_aliasing={{0}: (0, {}), {1}: (1, {}), {2}: (2, {})} | custom-call | tf_op jit(solution)/shard_map/sweep_turn/pallas_call | solution.py:499
  49.3 1.4 %collective-permute-start.7 = (f32[32,512]{1,0:T(8,128)S(1)}, f32[32,512]{1,0:T(8,128)S(1)}, u32[]{:S(2)}, u32[]{:S(2)}) collective-permute-start(f32[32,512]{1,0:T(8,128)S(1)} %get-tuple-element.75), channel_id=1, source_target_pairs={{0,8},{1,9},{2,10},{3,11},{4,12},{5,13},{6,14},{7,15}} | collective-permute-start | bytes 196616 | tf_op jit(solution)/shard_map/ppermute | solution.py:25
  50.8 1.9 %collective-permute-done.7.refs_3_ = f32[32,512]{1,0:T(8,128)S(1)} collective-permute-done((f32[32,512]{1,0:T(8,128)S(1)}, f32[32,512]{1,0:T(8,128)S(1)}, u32[]{:S(2)}, u32[]{:S(2)}) %collective-permute-start.7) | collective-permute-done | bytes 65568 | tf_op jit(solution)/shard_map/ppermute | solution.py:25
  52.6 0.7 collective-permute-start.8
  53.3 0.7 collective-permute-start.9
  54.2 0.7 collective-permute-start.10
  54.9 9.9 %joined_blocks.2 = (bf16[4,2,2,512,256]{4,3,2,1,0:T(8,128)(2,1)}, f32[4,256,256]{2,1,0:T(8,128)}) custom-call(f32[4,2,256,256]{3,2,1,0:T(8,128)} %bitcast.22, f32[4,2,512,256]{3,2,1,0:T(8,128)} %bitcast.19, s32[4,512]{1,0:T(4,128)S(1)} %bitcast.16, f32[4,256,256]{2,1,0:T(8,128)} %get-tuple-element.95.eliminated_hbm), custom_call_target="tpu_custom_call" | custom-call | flops 1 | bytes 1 | tf_op jit(solution)/shard_map/joined_blocks/pallas_call | solution.py:360
  64.9 0.7 collective-permute-start.11
  65.8 1.6 %collective-permute-start.12 = (f32[32,512]{1,0:T(8,128)S(1)}, f32[32,512]{1,0:T(8,128)S(1)}, u32[]{:S(2)}, u32[]{:S(2)}) collective-permute-start(f32[32,512]{1,0:T(8,128)S(1)} %get-tuple-element.106), channel_id=1, source_target_pairs={{8,0},{9,1},{10,2},{11,3},{12,4},{13,5},{14,6},{15,7}} | collective-permute-start | bytes 196616 | tf_op jit(solution)/shard_map/ppermute | solution.py:25
  67.3 20.1 %collective-permute-done.12.refs_3_ = f32[32,512]{1,0:T(8,128)S(1)} collective-permute-done((f32[32,512]{1,0:T(8,128)S(1)}, f32[32,512]{1,0:T(8,128)S(1)}, u32[]{:S(2)}, u32[]{:S(2)}) %collective-permute-start.12) | collective-permute-done | bytes 65568 | tf_op jit(solution)/shard_map/ppermute | solution.py:25
  87.4 2.0 %sweep_turn.13 = (f32[4,32,512]{2,1,0:T(8,128)S(1)}, f32[4,2,32,512]{3,2,1,0:T(8,128)S(1)}, bf16[4,2,1024,512]{3,2,1,0:T(8,128)(2,1)S(1)}, f32[32,512]{1,0:T(8,128)}) custom-call(f32[4,32,512]{2,1,0:T(8,128)S(1)} %get-tuple-element.103.refs_0_, ...), custom_call_target="tpu_custom_call", output_to_operand_aliasing={{0}: (0, {}), {1}: (1, {}), {2}: (2, {})} | custom-call | tf_op jit(solution)/shard_map/sweep_turn/pallas_call | solution.py:499
  89.4 13.0 %all_to_all.11.arrived_ref = f32[8,32,512]{2,1,0:T(8,128)S(1)} all-to-all(f32[8,32,512]{2,1,0:T(8,128)S(1)} %bitcast.10), channel_id=1, replica_groups={{0,1,2,3,4,5,6,7},{8,9,10,11,12,13,14,15},{16,17,18,19,20,21,22,23},{24..., dimensions={0} | all-to-all | bytes 1048576 | tf_op jit(solution)/shard_map/all_to_all | solution.py:533
  102.4 2.8 %finish.1 = (f32[4,2,256,128]{3,2,1,0:T(8,128)}, f32[2,512,128]{2,1,0:T(8,128)}) custom-call(f32[8,32,512]{2,1,0:T(8,128)S(1)} %all_to_all.11.arrived_ref, bf16[4,2,2,512,256]{4,3,2,1,0:T(8,128)(2,1)S(1)} %copy-done, f32[4,256,256]{2,1,0:T(8,128)S(1)} %copy-done.2), custom_call_target="tpu_custom_call" | custom-call | tf_op jit(solution)/shard_map/finish/pallas_call | solution.py:417
  (29 shorter events, 2.0 us)
Async XLA Ops:
  0.6 5.4 %collective-permute-start = (f32[1024,512]{1,0:T(8,128)}, f32[1024,512]{1,0:T(8,128)S(1)}, u32[]{:S(2)}, u32[]{:S(2)}) collective-permute-start(f32[1024,512]{1,0:T(8,128)} %bitcast.11), channel_id=1, source_target_pairs={{0,2},{1,3},{2,0},{3,1},{4,6},{5,7},{6,4},{7,5},{8,10},{9,11},{10,... | collective-permute-start | bytes 6291464 | tf_op jit(solution)/shard_map/ppermute | solution.py:25
  2.3 18.2 %collective-permute-start.1 = (f32[320,512]{1,0:T(8,128)S(1)}, f32[320,512]{1,0:T(8,128)S(1)}, u32[]{:S(2)}, u32[]{:S(2)}) collective-permute-start(f32[320,512]{1,0:T(8,128)S(1)} %constant_dynamic-slice_fusion), channel_id=1, source_target_pairs={{0,4},{1,5},{2,6},{3,7},{4,0},{5,1},{6,2},{7,3},{8,12},{9,13},{10,... | collective-permute-start | bytes 1966088 | tf_op jit(solution)/shard_map/ppermute | solution.py:25
  6.1 36.6 %collective-permute-start.3 = (f32[384,512]{1,0:T(8,128)S(1)}, f32[384,512]{1,0:T(8,128)S(1)}, u32[]{:S(2)}, u32[]{:S(2)}) collective-permute-start(f32[384,512]{1,0:T(8,128)S(1)} %slice.4), channel_id=1, source_target_pairs={{0,4},{1,5},{2,6},{3,7},{4,0},{5,1},{6,2},{7,3},{8,12},{9,13},{10,... | collective-permute-start | bytes 2359304 | tf_op jit(solution)/shard_map/ppermute | solution.py:25
  8.0 35.4 %copy-start.1 = (f32[1,2,512,512]{3,2,1,0:T(8,128)S(1)}, f32[1,2,512,512]{3,2,1,0:T(8,128)}, u32[]{:S(2)}) copy-start(f32[1,2,512,512]{3,2,1,0:T(8,128)} %param.13) | copy-start | bytes 6291460
  20.5 22.2 %collective-permute-start.2 = (f32[320,512]{1,0:T(8,128)S(1)}, f32[320,512]{1,0:T(8,128)S(1)}, u32[]{:S(2)}, u32[]{:S(2)}) collective-permute-start(f32[320,512]{1,0:T(8,128)S(1)} %collective-permute-done.1.refs_2_), channel_id=1, source_target_pairs={{0,1},{1,0},{2,3},{3,2},{4,5},{5,4},{6,7},{7,6},{8,9},{9,8},{10,11... | collective-permute-start | bytes 1966088 | tf_op jit(solution)/shard_map/ppermute | solution.py:25
  42.7 4.2 %collective-permute-start.6 = (f32[384,512]{1,0:T(8,128)S(1)}, f32[384,512]{1,0:T(8,128)S(1)}, u32[]{:S(2)}, u32[]{:S(2)}) collective-permute-start(f32[384,512]{1,0:T(8,128)S(1)} %collective-permute-done.3.refs_4_), channel_id=1, source_target_pairs={{0,2},{1,3},{2,0},{3,1},{4,6},{5,7},{6,4},{7,5},{8,10},{9,11},{10,... | collective-permute-start | bytes 2359304 | tf_op jit(solution)/shard_map/ppermute | solution.py:25
  42.9 3.1 %collective-permute-start.4 = (f32[320,512]{1,0:T(8,128)S(1)}, f32[320,512]{1,0:T(8,128)S(1)}, u32[]{:S(2)}, u32[]{:S(2)}) collective-permute-start(f32[320,512]{1,0:T(8,128)S(1)} %collective-permute-done.1.refs_2_), channel_id=1, source_target_pairs={{0,2},{1,3},{2,0},{3,1},{4,6},{5,7},{6,4},{7,5},{8,10},{9,11},{10,... | collective-permute-start | bytes 1966088 | tf_op jit(solution)/shard_map/ppermute | solution.py:25
  43.2 3.6 %collective-permute-start.5 = (f32[320,512]{1,0:T(8,128)S(1)}, f32[320,512]{1,0:T(8,128)S(1)}, u32[]{:S(2)}, u32[]{:S(2)}) collective-permute-start(f32[320,512]{1,0:T(8,128)S(1)} %collective-permute-done.2.refs_3_), channel_id=1, source_target_pairs={{0,2},{1,3},{2,0},{3,1},{4,6},{5,7},{6,4},{7,5},{8,10},{9,11},{10,... | collective-permute-start | bytes 1966088 | tf_op jit(solution)/shard_map/ppermute | solution.py:25
  49.3 3.3 %collective-permute-start.7 = (f32[32,512]{1,0:T(8,128)S(1)}, f32[32,512]{1,0:T(8,128)S(1)}, u32[]{:S(2)}, u32[]{:S(2)}) collective-permute-start(f32[32,512]{1,0:T(8,128)S(1)} %get-tuple-element.75), channel_id=1, source_target_pairs={{0,8},{1,9},{2,10},{3,11},{4,12},{5,13},{6,14},{7,15}} | collective-permute-start | bytes 196616 | tf_op jit(solution)/shard_map/ppermute | solution.py:25
  52.6 0.7 collective-permute-start.8
  53.3 0.7 collective-permute-start.9
  54.0 0.9 copy-start.3
  54.2 10.6 %collective-permute-start.10 = (f32[32,512]{1,0:T(8,128)S(1)}, f32[32,512]{1,0:T(8,128)S(1)}, u32[]{:S(2)}, u32[]{:S(2)}) collective-permute-start(f32[32,512]{1,0:T(8,128)S(1)} %get-tuple-element.85), channel_id=1, source_target_pairs={{24,16},{25,17},{26,18},{27,19},{28,20},{29,21},{30,22},{31,23}} | collective-permute-start | bytes 196616 | tf_op jit(solution)/shard_map/ppermute | solution.py:25
  64.9 0.8 collective-permute-start.11
  65.7 36.7 %copy-start = (bf16[4,2,2,512,256]{4,3,2,1,0:T(8,128)(2,1)S(1)}, bf16[4,2,2,512,256]{4,3,2,1,0:T(8,128)(2,1)}, u32[]{:S(2)}) copy-start(bf16[4,2,2,512,256]{4,3,2,1,0:T(8,128)(2,1)} %get-tuple-element.108.joined_ref) | copy-start | bytes 12582916
  65.7 36.7 %copy-start.2 = (f32[4,256,256]{2,1,0:T(8,128)S(1)}, f32[4,256,256]{2,1,0:T(8,128)}, u32[]{:S(2)}) copy-start(f32[4,256,256]{2,1,0:T(8,128)} %get-tuple-element.109.plain_ref) | copy-start | bytes 3145732
  65.8 21.7 %collective-permute-start.12 = (f32[32,512]{1,0:T(8,128)S(1)}, f32[32,512]{1,0:T(8,128)S(1)}, u32[]{:S(2)}, u32[]{:S(2)}) collective-permute-start(f32[32,512]{1,0:T(8,128)S(1)} %get-tuple-element.106), channel_id=1, source_target_pairs={{8,0},{9,1},{10,2},{11,3},{12,4},{13,5},{14,6},{15,7}} | collective-permute-start | bytes 196616 | tf_op jit(solution)/shard_map/ppermute | solution.py:25
